TPU v7x, 32 devices: a whole 2x2x4 slice. The times are simulated.
32 devices in a mesh: groups: 2 (over y), space: 4 (over z), probe: 4 (over x, core).
Axes of the slice: x: 2, y: 2, z: 4, core: 2. Of those that a mesh axis runs over, the one named last changes fastest.
Arguments:
- probe_amplitudes: float32 [8, 12, 64, 256], P(('groups', 'probe'), 'space'), parts along dimension 0, may hold values from -4 to 4
- site_mask: float32 [24, 64, 256], P(('groups', 'space')), parts along dimension 0, may hold values from 0 to 1, as said below
- couplings: float32 [3, 24, 64, 256], P(None, ('groups', 'space')), parts along dimension 1, may hold values from 0.3 to 1.5
- target: float32 [512], P('groups'), parts along dimension 0, may hold values from -3 to 3
Outputs:
- probe_costate: float32 [8, 12, 64, 256], P(('groups', 'probe'), 'space'), parts along dimension 0
- bond_grad: float32 [3, 24, 64, 256], P(None, ('groups', 'space'), 'probe'), parts along dimension 1
There are 2 independent parts, one for each index of `groups`. A program takes and returns all parts, laid end to end along the dimension named above; each array names one. Nothing has to cross between parts.
Inputs may be any that keep to these rules, and one draw needn't show every extreme that they name: `site_mask`: 0 at a vacancy, at least 0.4 where a spin is present.
All inputs are finite; a program needn't handle non-finite values.
Results may differ from a plain program's by a relative error of at most 0.0003.
Values sent between devices are 32-bit elements; how exact they have to be, the bound alone decides.
A program may use at most 64 MiB of HBM per device.

v0:
```python
import jax
import jax.numpy as jnp
from jax import lax
from jax.sharding import PartitionSpec as P

STEPS = 8


SCALE = 10.0


def extended(block, sides, width):
    for axis, dim in sides:
        count = lax.axis_size(axis)
        forward = [(i, i + 1) for i in range(count - 1)]
        forward.append((count - 1, 0))
        backward = [(target, source) for source, target in forward]
        low = lax.ppermute(
            lax.slice_in_dim(block, block.shape[dim] - width, None, axis=dim), axis, forward
        )
        high = lax.ppermute(lax.slice_in_dim(block, 0, width, axis=dim), axis, backward)
        block = jnp.concatenate([low, block, high], axis=dim)
    return block


def kernel_table(count, points):
    order = jnp.arange(count).astype(jnp.float32)
    theta = jnp.pi * (jnp.arange(points).astype(jnp.float32) + 0.5) / points
    table = jnp.cos(order[:, None] * theta[None, :])
    total = count + 1.0
    jackson = (
        (total - order) * jnp.cos(jnp.pi * order / total)
        + jnp.sin(jnp.pi * order / total) / jnp.tan(jnp.pi / total)
    ) / total
    doubled = jnp.where(jnp.arange(count) > 0, 2.0, 1.0).astype(jnp.float32)
    return (table, doubled * jackson)


def misfit_weights(moments, target):
    table, scaled = kernel_table(moments.shape[0], target.shape[0])
    spectrum = jnp.dot(scaled * moments, table, precision=lax.Precision.HIGHEST)
    misfit = spectrum - target
    return 2.0 / target.shape[0] * scaled * jnp.dot(table, misfit, precision=lax.Precision.HIGHEST)


def trimmed(bonds, margin):
    planes = bonds[0].shape[0] - 4
    return tuple((bond[2 - margin : 2 + planes + margin] for bond in bonds))


def apply_field(padded, bonds):
    centre = padded[1:-1]
    total = bonds[0][1:-1] * (centre - padded[2:]) + bonds[0][:-2] * (centre - padded[:-2])
    for axis in (1, 2):
        inside = bonds[axis][1:-1]
        total = (
            total
            + inside * (centre - jnp.roll(centre, -1, axis))
            + jnp.roll(inside, 1, axis) * (centre - jnp.roll(centre, 1, axis))
        )
    return total / SCALE - centre


def bond_products(adjoint, state):
    centre_adj = adjoint[1:-1]
    centre_state = state[1:-1]
    along_first = (centre_adj - adjoint[2:]) * (centre_state - state[2:])
    along_second = (centre_adj - jnp.roll(centre_adj, -1, 1)) * (
        centre_state - jnp.roll(centre_state, -1, 1)
    )
    along_third = (centre_adj - jnp.roll(centre_adj, -1, 2)) * (
        centre_state - jnp.roll(centre_state, -1, 2)
    )
    return jnp.stack([along_first, along_second, along_third])


def on_device(probe_amplitudes, site_mask, couplings, target):
    stacked = jnp.concatenate([site_mask[None], couplings], 0)
    wide = extended(stacked, (("space", 1),), 3)
    outer = wide[0]
    inner = outer[1:-1]
    joined = wide[1:, 1:-1]
    bonds = (
        joined[0] * inner * outer[2:],
        joined[1] * inner * jnp.roll(inner, -1, 1),
        joined[2] * inner * jnp.roll(inner, -1, 2),
    )
    probe = probe_amplitudes[0] * site_mask
    fields = []
    value = probe
    previous = probe
    for step in range(STEPS):
        padded = extended(value, (("space", 0),), 1)
        fields.append(padded)
        image = apply_field(padded, trimmed(bonds, 1))
        following = image if step == 0 else 2.0 * image - previous
        previous = value
        value = following
    chain_states = [padded_state[1:-1] for padded_state in fields] + [value]
    count = (
        lax.axis_size("probe")
        * probe_amplitudes.shape[0]
        * lax.axis_size("space")
        * site_mask.shape[0]
        * site_mask.shape[1]
        * site_mask.shape[2]
    )
    totals = jnp.stack(
        [lax.psum(jnp.sum(probe * state), ("space", "probe")) for state in chain_states]
    )
    moments = totals / count
    weights = misfit_weights(moments, target)
    products = jnp.zeros(couplings.shape, jnp.float32)
    later = weights[STEPS] * probe
    beyond = later
    for step in range(STEPS, 0, -1):
        padded_adj = extended(later, (("space", 0),), 1)
        image = apply_field(padded_adj, trimmed(bonds, 1))
        factor = 1.0 if step == 1 else 2.0
        products = products + factor * bond_products(padded_adj, fields[step - 1])
        if step == STEPS:
            earlier = weights[step - 1] * probe + 2.0 * image
        elif step == 1:
            earlier = weights[0] * probe + image - beyond
        else:
            earlier = weights[step - 1] * probe + 2.0 * image - beyond
        beyond = later
        later = earlier
    costate = later
    for step in range(STEPS + 1):
        costate = costate + weights[step] * chain_states[step]
    pairs = jnp.stack(
        [
            site_mask * outer[4:-2],
            site_mask * jnp.roll(site_mask, -1, 1),
            site_mask * jnp.roll(site_mask, -1, 2),
        ]
    )
    local_grad = pairs * products / SCALE
    bond_grad = lax.psum_scatter(local_grad, "probe", scatter_dimension=2, tiled=True)
    return (costate[None], bond_grad)


def solution(mesh):
    return jax.shard_map(
        on_device,
        mesh=mesh,
        in_specs=(
            P(("groups", "probe"), "space", None, None),
            P(("groups", "space"), None, None),
            P(None, ("groups", "space"), None, None),
            P("groups"),
        ),
        out_specs=(
            P(("groups", "probe"), "space", None, None),
            P(None, ("groups", "space"), "probe", None),
        ),
        check_vma=False,
    )
```

profile of v0, /device:TPU:0, one launch (start us, length us, event | category | flops | bytes accessed | tf_op | source)
XLA Modules:
  0.0 245.0 jit_solution(2992943560017267455)
XLA Ops:
  8.4 5.1 %collective-permute-start.1 = (f32[4,3,64,256]{3,2,1,0:T(8,128)S(1)}, f32[4,3,64,256]{3,2,1,0:T(8,128)S(1)}, u32[]{:S(2)}, u32[]{:S(2)}) collective-permute-start(f32[4,3,64,256]{3,2,1,0:T(8,128)S(1)} %pad_maximum_fusion), channel_id=1, source_target_pairs={{4,0},{8,4},{12,8},{0,12},{5,1},{9,5},{13,9},{1,13},{6,2},{10,6},{... | collective-permute-start | bytes 2359304 | tf_op jit(solution)/shard_map/ppermute | solution.py:21
  14.9 16.6 %collective-permute-done.1 = f32[4,3,64,256]{3,2,1,0:T(8,128)S(1)} collective-permute-done((f32[4,3,64,256]{3,2,1,0:T(8,128)S(1)}, f32[4,3,64,256]{3,2,1,0:T(8,128)S(1)}, u32[]{:S(2)}, u32[]{:S(2)}) %collective-permute-start.1) | collective-permute-done | bytes 786464 | tf_op jit(solution)/shard_map/ppermute | solution.py:21
  32.6 15.4 %collective-permute-done = f32[4,3,64,256]{3,2,1,0:T(8,128)S(1)} collective-permute-done((f32[4,3,64,256]{3,2,1,0:T(8,128)S(1)}, f32[4,3,64,256]{3,2,1,0:T(8,128)S(1)}, u32[]{:S(2)}, u32[]{:S(2)}) %collective-permute-start) | collective-permute-done | bytes 786464 | tf_op jit(solution)/shard_map/ppermute | solution.py:18
  52.5 2.2 collective-permute-done.2
  54.7 3.6 %collective-permute-done.3 = f32[1,64,256]{2,1,0:T(8,128)S(1)} collective-permute-done((f32[1,64,256]{2,1,0:T(8,128)S(1)}, f32[1,64,256]{2,1,0:T(8,128)S(1)}, u32[]{:S(2)}, u32[]{:S(2)}) %collective-permute-start.3) | collective-permute-done | bytes 65568 | tf_op jit(solution)/shard_map/ppermute | solution.py:18
  61.0 2.2 collective-permute-done.4
  63.3 2.3 collective-permute-done.5
  68.2 2.2 collective-permute-done.6
  75.1 2.9 %collective-permute-done.8 = f32[1,64,256]{2,1,0:T(8,128)S(1)} collective-permute-done((f32[1,64,256]{2,1,0:T(8,128)S(1)}, f32[1,64,256]{2,1,0:T(8,128)S(1)}, u32[]{:S(2)}, u32[]{:S(2)}) %collective-permute-start.8) | collective-permute-done | bytes 65568 | tf_op jit(solution)/shard_map/ppermute | solution.py:21
  82.5 2.2 collective-permute-done.10
  84.7 2.6 %collective-permute-done.11 = f32[1,64,256]{2,1,0:T(8,128)S(1)} collective-permute-done((f32[1,64,256]{2,1,0:T(8,128)S(1)}, f32[1,64,256]{2,1,0:T(8,128)S(1)}, u32[]{:S(2)}, u32[]{:S(2)}) %collective-permute-start.11) | collective-permute-done | bytes 65568 | tf_op jit(solution)/shard_map/ppermute | solution.py:18
  90.0 2.9 %collective-permute-done.12 = f32[1,64,256]{2,1,0:T(8,128)S(1)} collective-permute-done((f32[1,64,256]{2,1,0:T(8,128)S(1)}, f32[1,64,256]{2,1,0:T(8,128)S(1)}, u32[]{:S(2)}, u32[]{:S(2)}) %collective-permute-start.12) | collective-permute-done | bytes 65568 | tf_op jit(solution)/shard_map/ppermute | solution.py:21
  97.6 2.4 collective-permute-done.14
  100.0 2.0 collective-permute-done.15
  104.7 2.2 collective-permute-done.16
  106.9 2.2 collective-permute-done.17
  110.9 30.7 %all-reduce = (f32[1]{0:T(128)}, f32[1]{0:T(128)}, f32[1]{0:T(128)}, f32[1]{0:T(128)}, f32[1]{0:T(128)}, /*index=5*/f32[1]{0:T(128)}, f32[1]{0:T(128)}, f32[1]{0:T(128)}, f32[1]{0:T(128)}) all-reduce(f32[1]{0:T(128)} %bitcast.1, f32[1]{0:T(128)} %bitcast.8, ...), channel_id=1, replica_groups=mesh['groups'=2,'space'=4,'probe'=4] {'space','probe'}, use_global_device_ids=true, to_apply=%region_1.2 | all-reduce | flops 9 | bytes 72 | tf_op jit(solution)/shard_map/psum | solution.py:109
  141.6 6.2 %stack.147 = f32[9]{0:T(128)} concatenate(f32[1]{0:T(128)} %get-tuple-element.11, f32[1]{0:T(128)} %get-tuple-element.12, f32[1]{0:T(128)} %get-tuple-element.13, f32[1]{0:T(128)} %get-tuple-element.14, f32[1]{0:T(128)} %get-tuple-element.15, f32[1]{0:T(128)} %get-tuple-element.16, f32[1]{0:T(128)} %get-tuple-element.17, f32[1]{0:T(128)} %get-tuple-element.18, f32[1]{0:T(128)} %get-tuple-element.19), dimensions={0} | concatenate | bytes 72 | tf_op jit(solution)/shard_map/stack | solution.py:108
  154.1 2.2 collective-permute-done.18
  170.4 2.2 collective-permute-done.22
  172.6 2.5 %collective-permute-done.23 = f32[1,64,256]{2,1,0:T(8,128)S(1)} collective-permute-done((f32[1,64,256]{2,1,0:T(8,128)S(1)}, f32[1,64,256]{2,1,0:T(8,128)S(1)}, u32[]{:S(2)}, u32[]{:S(2)}) %collective-permute-start.23) | collective-permute-done | bytes 65568 | tf_op jit(solution)/shard_map/ppermute | solution.py:18
  178.6 2.1 collective-permute-done.24
  180.7 2.2 collective-permute-done.25
  186.3 2.4 collective-permute-done.26
  193.7 2.6 %collective-permute-done.28 = f32[1,64,256]{2,1,0:T(8,128)S(1)} collective-permute-done((f32[1,64,256]{2,1,0:T(8,128)S(1)}, f32[1,64,256]{2,1,0:T(8,128)S(1)}, u32[]{:S(2)}, u32[]{:S(2)}) %collective-permute-start.28) | collective-permute-done | bytes 65568 | tf_op jit(solution)/shard_map/ppermute | solution.py:21
  196.3 2.0 collective-permute-done.29
  201.9 2.1 collective-permute-done.30
  203.9 2.8 %collective-permute-done.31 = f32[1,64,256]{2,1,0:T(8,128)S(1)} collective-permute-done((f32[1,64,256]{2,1,0:T(8,128)S(1)}, f32[1,64,256]{2,1,0:T(8,128)S(1)}, u32[]{:S(2)}, u32[]{:S(2)}) %collective-permute-start.31) | collective-permute-done | bytes 65568 | tf_op jit(solution)/shard_map/ppermute | solution.py:18
  211.2 3.7 %collective-permute-done.32 = f32[1,64,256]{2,1,0:T(8,128)S(1)} collective-permute-done((f32[1,64,256]{2,1,0:T(8,128)S(1)}, f32[1,64,256]{2,1,0:T(8,128)S(1)}, u32[]{:S(2)}, u32[]{:S(2)}) %collective-permute-start.32) | collective-permute-done | bytes 65568 | tf_op jit(solution)/shard_map/ppermute | solution.py:21
  217.4 6.3 %collective-permute-done.33 = f32[1,64,256]{2,1,0:T(8,128)S(1)} collective-permute-done((f32[1,64,256]{2,1,0:T(8,128)}, f32[1,64,256]{2,1,0:T(8,128)S(1)}, u32[]{:S(2)}, u32[]{:S(2)}) %collective-permute-start.33) | collective-permute-done | bytes 65568 | tf_op jit(solution)/shard_map/ppermute | solution.py:18
  223.6 8.3 %fusion.258 = f32[1,3,64,256]{3,2,1,0:T(8,128)} fusion(f32[3,64,256]{2,1,0:T(8,128)} %get-tuple-element.20, f32[3,64,256]{2,1,0:T(8,128)S(1)} %fusion.152, f32[3,64,256]{2,1,0:T(8,128)S(1)} %fusion.164, f32[3,64,256]{2,1,0:T(8,128)S(1)} %fusion.176, f32[3,64,256]{2,1,0:T(8,128)S(1)} %fusion.188, f32[3,64,256]{2,1,0:T(8,128)S(1)} %fusion.200, ...), kind=kLoop, calls=%fused_computation.405 | loop fusion | flops 2260992 | bytes 4456484 | tf_op jit(solution)/shard_map/broadcast_in_dim | solution.py:141
  231.9 6.3 %reduce-scatter.2.cloned.1.call-done = f32[3,3,16,256]{3,2,1,0:T(8,128)} async-done(((f32[3,3,64,256]{3,2,1,0:T(8,128)}), f32[3,3,16,256]{3,2,1,0:T(8,128)}) %reduce-scatter.2.cloned.1.call-update) | async-done | bytes 147472 | tf_op jit(solution)/shard_map/reduce_scatter | solution.py:140
  (346 shorter events, 75.8 us)
Async XLA Ops:
  7.2 231.0 %reduce-scatter.2.cloned.1.call-start = ((), (), s32[]{:S(2)}) async-start(), calls=%async_computation.1 | async-start | bytes 737280 | tf_op jit(solution)/shard_map/reduce_scatter | solution.py:140
  8.4 23.1 %collective-permute-start.1 = (f32[4,3,64,256]{3,2,1,0:T(8,128)S(1)}, f32[4,3,64,256]{3,2,1,0:T(8,128)S(1)}, u32[]{:S(2)}, u32[]{:S(2)}) collective-permute-start(f32[4,3,64,256]{3,2,1,0:T(8,128)S(1)} %pad_maximum_fusion), channel_id=1, source_target_pairs={{4,0},{8,4},{12,8},{0,12},{5,1},{9,5},{13,9},{1,13},{6,2},{10,6},{... | collective-permute-start | bytes 2359304 | tf_op jit(solution)/shard_map/ppermute | solution.py:21
  13.5 34.6 %collective-permute-start = (f32[4,3,64,256]{3,2,1,0:T(8,128)S(1)}, f32[4,3,64,256]{3,2,1,0:T(8,128)S(1)}, u32[]{:S(2)}, u32[]{:S(2)}) collective-permute-start(f32[4,3,64,256]{3,2,1,0:T(8,128)S(1)} %pad_maximum_fusion), channel_id=1, source_target_pairs={{0,4},{4,8},{8,12},{12,0},{1,5},{5,9},{9,13},{13,1},{2,6},{6,10},{... | collective-permute-start | bytes 2359304 | tf_op jit(solution)/shard_map/ppermute | solution.py:18
  50.4 4.3 %collective-permute-start.2 = (f32[1,64,256]{2,1,0:T(8,128)S(1)}, f32[1,64,256]{2,1,0:T(8,128)S(1)}, u32[]{:S(2)}, u32[]{:S(2)}) collective-permute-start(f32[1,64,256]{2,1,0:T(8,128)S(1)} %get-tuple-element.209), channel_id=1, source_target_pairs={{4,0},{8,4},{12,8},{0,12},{5,1},{9,5},{13,9},{1,13},{6,2},{10,6},{... | collective-permute-start | bytes 196616 | tf_op jit(solution)/shard_map/ppermute | solution.py:21
  52.2 6.2 %collective-permute-start.3 = (f32[1,64,256]{2,1,0:T(8,128)S(1)}, f32[1,64,256]{2,1,0:T(8,128)S(1)}, u32[]{:S(2)}, u32[]{:S(2)}) collective-permute-start(f32[1,64,256]{2,1,0:T(8,128)S(1)} %get-tuple-element.210), channel_id=1, source_target_pairs={{0,4},{4,8},{8,12},{12,0},{1,5},{5,9},{9,13},{13,1},{2,6},{6,10},{... | collective-permute-start | bytes 196616 | tf_op jit(solution)/shard_map/ppermute | solution.py:18
  58.9 4.3 %collective-permute-start.4 = (f32[1,64,256]{2,1,0:T(8,128)S(1)}, f32[1,64,256]{2,1,0:T(8,128)S(1)}, u32[]{:S(2)}, u32[]{:S(2)}) collective-permute-start(f32[1,64,256]{2,1,0:T(8,128)S(1)} %get-tuple-element.199), channel_id=1, source_target_pairs={{4,0},{8,4},{12,8},{0,12},{5,1},{9,5},{13,9},{1,13},{6,2},{10,6},{... | collective-permute-start | bytes 196616 | tf_op jit(solution)/shard_map/ppermute | solution.py:21
  59.3 6.3 %collective-permute-start.5 = (f32[1,64,256]{2,1,0:T(8,128)S(1)}, f32[1,64,256]{2,1,0:T(8,128)S(1)}, u32[]{:S(2)}, u32[]{:S(2)}) collective-permute-start(f32[1,64,256]{2,1,0:T(8,128)S(1)} %get-tuple-element.200), channel_id=1, source_target_pairs={{0,4},{4,8},{8,12},{12,0},{1,5},{5,9},{9,13},{13,1},{2,6},{6,10},{... | collective-permute-start | bytes 196616 | tf_op jit(solution)/shard_map/ppermute | solution.py:18
  66.1 4.3 %collective-permute-start.6 = (f32[1,64,256]{2,1,0:T(8,128)S(1)}, f32[1,64,256]{2,1,0:T(8,128)S(1)}, u32[]{:S(2)}, u32[]{:S(2)}) collective-permute-start(f32[1,64,256]{2,1,0:T(8,128)S(1)} %get-tuple-element.189), channel_id=1, source_target_pairs={{4,0},{8,4},{12,8},{0,12},{5,1},{9,5},{13,9},{1,13},{6,2},{10,6},{... | collective-permute-start | bytes 196616 | tf_op jit(solution)/shard_map/ppermute | solution.py:21
  66.3 6.1 %collective-permute-start.7 = (f32[1,64,256]{2,1,0:T(8,128)S(1)}, f32[1,64,256]{2,1,0:T(8,128)S(1)}, u32[]{:S(2)}, u32[]{:S(2)}) collective-permute-start(f32[1,64,256]{2,1,0:T(8,128)S(1)} %get-tuple-element.190), channel_id=1, source_target_pairs={{0,4},{4,8},{8,12},{12,0},{1,5},{5,9},{9,13},{13,1},{2,6},{6,10},{... | collective-permute-start | bytes 196616 | tf_op jit(solution)/shard_map/ppermute | solution.py:18
  73.0 5.0 %collective-permute-start.8 = (f32[1,64,256]{2,1,0:T(8,128)S(1)}, f32[1,64,256]{2,1,0:T(8,128)S(1)}, u32[]{:S(2)}, u32[]{:S(2)}) collective-permute-start(f32[1,64,256]{2,1,0:T(8,128)S(1)} %get-tuple-element.179), channel_id=1, source_target_pairs={{4,0},{8,4},{12,8},{0,12},{5,1},{9,5},{13,9},{1,13},{6,2},{10,6},{... | collective-permute-start | bytes 196616 | tf_op jit(solution)/shard_map/ppermute | solution.py:21
  73.4 6.4 %collective-permute-start.9 = (f32[1,64,256]{2,1,0:T(8,128)S(1)}, f32[1,64,256]{2,1,0:T(8,128)S(1)}, u32[]{:S(2)}, u32[]{:S(2)}) collective-permute-start(f32[1,64,256]{2,1,0:T(8,128)S(1)} %get-tuple-element.180), channel_id=1, source_target_pairs={{0,4},{4,8},{8,12},{12,0},{1,5},{5,9},{9,13},{13,1},{2,6},{6,10},{... | collective-permute-start | bytes 196616 | tf_op jit(solution)/shard_map/ppermute | solution.py:18
  80.4 4.3 %collective-permute-start.10 = (f32[1,64,256]{2,1,0:T(8,128)S(1)}, f32[1,64,256]{2,1,0:T(8,128)S(1)}, u32[]{:S(2)}, u32[]{:S(2)}) collective-permute-start(f32[1,64,256]{2,1,0:T(8,128)S(1)} %get-tuple-element.169), channel_id=1, source_target_pairs={{4,0},{8,4},{12,8},{0,12},{5,1},{9,5},{13,9},{1,13},{6,2},{10,6},{... | collective-permute-start | bytes 196616 | tf_op jit(solution)/shard_map/ppermute | solution.py:21
  81.3 6.1 %collective-permute-start.11 = (f32[1,64,256]{2,1,0:T(8,128)S(1)}, f32[1,64,256]{2,1,0:T(8,128)S(1)}, u32[]{:S(2)}, u32[]{:S(2)}) collective-permute-start(f32[1,64,256]{2,1,0:T(8,128)S(1)} %get-tuple-element.170), channel_id=1, source_target_pairs={{0,4},{4,8},{8,12},{12,0},{1,5},{5,9},{9,13},{13,1},{2,6},{6,10},{... | collective-permute-start | bytes 196616 | tf_op jit(solution)/shard_map/ppermute | solution.py:18
  87.9 5.0 %collective-permute-start.12 = (f32[1,64,256]{2,1,0:T(8,128)S(1)}, f32[1,64,256]{2,1,0:T(8,128)S(1)}, u32[]{:S(2)}, u32[]{:S(2)}) collective-permute-start(f32[1,64,256]{2,1,0:T(8,128)S(1)} %get-tuple-element.159), channel_id=1, source_target_pairs={{4,0},{8,4},{12,8},{0,12},{5,1},{9,5},{13,9},{1,13},{6,2},{10,6},{... | collective-permute-start | bytes 196616 | tf_op jit(solution)/shard_map/ppermute | solution.py:21
  88.8 6.1 %collective-permute-start.13 = (f32[1,64,256]{2,1,0:T(8,128)S(1)}, f32[1,64,256]{2,1,0:T(8,128)S(1)}, u32[]{:S(2)}, u32[]{:S(2)}) collective-permute-start(f32[1,64,256]{2,1,0:T(8,128)S(1)} %get-tuple-element.160), channel_id=1, source_target_pairs={{0,4},{4,8},{8,12},{12,0},{1,5},{5,9},{9,13},{13,1},{2,6},{6,10},{... | collective-permute-start | bytes 196616 | tf_op jit(solution)/shard_map/ppermute | solution.py:18
  95.5 4.5 %collective-permute-start.14 = (f32[1,64,256]{2,1,0:T(8,128)S(1)}, f32[1,64,256]{2,1,0:T(8,128)S(1)}, u32[]{:S(2)}, u32[]{:S(2)}) collective-permute-start(f32[1,64,256]{2,1,0:T(8,128)S(1)} %get-tuple-element.149), channel_id=1, source_target_pairs={{4,0},{8,4},{12,8},{0,12},{5,1},{9,5},{13,9},{1,13},{6,2},{10,6},{... | collective-permute-start | bytes 196616 | tf_op jit(solution)/shard_map/ppermute | solution.py:21
  95.9 6.1 %collective-permute-start.15 = (f32[1,64,256]{2,1,0:T(8,128)S(1)}, f32[1,64,256]{2,1,0:T(8,128)S(1)}, u32[]{:S(2)}, u32[]{:S(2)}) collective-permute-start(f32[1,64,256]{2,1,0:T(8,128)S(1)} %get-tuple-element.150), channel_id=1, source_target_pairs={{0,4},{4,8},{8,12},{12,0},{1,5},{5,9},{9,13},{13,1},{2,6},{6,10},{... | collective-permute-start | bytes 196616 | tf_op jit(solution)/shard_map/ppermute | solution.py:18
  102.6 4.3 %collective-permute-start.16 = (f32[1,64,256]{2,1,0:T(8,128)S(1)}, f32[1,64,256]{2,1,0:T(8,128)S(1)}, u32[]{:S(2)}, u32[]{:S(2)}) collective-permute-start(f32[1,64,256]{2,1,0:T(8,128)S(1)} %get-tuple-element.131), channel_id=1, source_target_pairs={{4,0},{8,4},{12,8},{0,12},{5,1},{9,5},{13,9},{1,13},{6,2},{10,6},{... | collective-permute-start | bytes 196616 | tf_op jit(solution)/shard_map/ppermute | solution.py:21
  103.0 6.1 %collective-permute-start.17 = (f32[1,64,256]{2,1,0:T(8,128)S(1)}, f32[1,64,256]{2,1,0:T(8,128)S(1)}, u32[]{:S(2)}, u32[]{:S(2)}) collective-permute-start(f32[1,64,256]{2,1,0:T(8,128)S(1)} %get-tuple-element.132), channel_id=1, source_target_pairs={{0,4},{4,8},{8,12},{12,0},{1,5},{5,9},{9,13},{13,1},{2,6},{6,10},{... | collective-permute-start | bytes 196616 | tf_op jit(solution)/shard_map/ppermute | solution.py:18
  152.0 4.3 %collective-permute-start.18 = (f32[1,64,256]{2,1,0:T(8,128)S(1)}, f32[1,64,256]{2,1,0:T(8,128)S(1)}, u32[]{:S(2)}, u32[]{:S(2)}) collective-permute-start(f32[1,64,256]{2,1,0:T(8,128)S(1)} %get-tuple-element.129), channel_id=1, source_target_pairs={{4,0},{8,4},{12,8},{0,12},{5,1},{9,5},{13,9},{1,13},{6,2},{10,6},{... | collective-permute-start | bytes 196616 | tf_op jit(solution)/shard_map/ppermute | solution.py:21
  152.1 6.1 %collective-permute-start.19 = (f32[1,64,256]{2,1,0:T(8,128)S(1)}, f32[1,64,256]{2,1,0:T(8,128)S(1)}, u32[]{:S(2)}, u32[]{:S(2)}) collective-permute-start(f32[1,64,256]{2,1,0:T(8,128)S(1)} %get-tuple-element.130), channel_id=1, source_target_pairs={{0,4},{4,8},{8,12},{12,0},{1,5},{5,9},{9,13},{13,1},{2,6},{6,10},{... | collective-permute-start | bytes 196616 | tf_op jit(solution)/shard_map/ppermute | solution.py:18
  160.1 4.8 %collective-permute-start.20 = (f32[1,64,256]{2,1,0:T(8,128)S(1)}, f32[1,64,256]{2,1,0:T(8,128)S(1)}, u32[]{:S(2)}, u32[]{:S(2)}) collective-permute-start(f32[1,64,256]{2,1,0:T(8,128)S(1)} %get-tuple-element.119), channel_id=1, source_target_pairs={{4,0},{8,4},{12,8},{0,12},{5,1},{9,5},{13,9},{1,13},{6,2},{10,6},{... | collective-permute-start | bytes 196616 | tf_op jit(solution)/shard_map/ppermute | solution.py:21
  160.2 6.1 %collective-permute-start.21 = (f32[1,64,256]{2,1,0:T(8,128)S(1)}, f32[1,64,256]{2,1,0:T(8,128)S(1)}, u32[]{:S(2)}, u32[]{:S(2)}) collective-permute-start(f32[1,64,256]{2,1,0:T(8,128)S(1)} %get-tuple-element.120), channel_id=1, source_target_pairs={{0,4},{4,8},{8,12},{12,0},{1,5},{5,9},{9,13},{13,1},{2,6},{6,10},{... | collective-permute-start | bytes 196616 | tf_op jit(solution)/shard_map/ppermute | solution.py:18
  168.2 4.4 %collective-permute-start.22 = (f32[1,64,256]{2,1,0:T(8,128)S(1)}, f32[1,64,256]{2,1,0:T(8,128)S(1)}, u32[]{:S(2)}, u32[]{:S(2)}) collective-permute-start(f32[1,64,256]{2,1,0:T(8,128)S(1)} %get-tuple-element.109), channel_id=1, source_target_pairs={{4,0},{8,4},{12,8},{0,12},{5,1},{9,5},{13,9},{1,13},{6,2},{10,6},{... | collective-permute-start | bytes 196616 | tf_op jit(solution)/shard_map/ppermute | solution.py:21
  168.9 6.2 %collective-permute-start.23 = (f32[1,64,256]{2,1,0:T(8,128)S(1)}, f32[1,64,256]{2,1,0:T(8,128)S(1)}, u32[]{:S(2)}, u32[]{:S(2)}) collective-permute-start(f32[1,64,256]{2,1,0:T(8,128)S(1)} %get-tuple-element.110), channel_id=1, source_target_pairs={{0,4},{4,8},{8,12},{12,0},{1,5},{5,9},{9,13},{13,1},{2,6},{6,10},{... | collective-permute-start | bytes 196616 | tf_op jit(solution)/shard_map/ppermute | solution.py:18
  176.4 6.5 %collective-permute-start.25 = (f32[1,64,256]{2,1,0:T(8,128)S(1)}, f32[1,64,256]{2,1,0:T(8,128)S(1)}, u32[]{:S(2)}, u32[]{:S(2)}) collective-permute-start(f32[1,64,256]{2,1,0:T(8,128)S(1)} %get-tuple-element.100), channel_id=1, source_target_pairs={{0,4},{4,8},{8,12},{12,0},{1,5},{5,9},{9,13},{13,1},{2,6},{6,10},{... | collective-permute-start | bytes 196616 | tf_op jit(solution)/shard_map/ppermute | solution.py:18
  184.1 4.7 %collective-permute-start.26 = (f32[1,64,256]{2,1,0:T(8,128)S(1)}, f32[1,64,256]{2,1,0:T(8,128)S(1)}, u32[]{:S(2)}, u32[]{:S(2)}) collective-permute-start(f32[1,64,256]{2,1,0:T(8,128)S(1)} %get-tuple-element.89), channel_id=1, source_target_pairs={{4,0},{8,4},{12,8},{0,12},{5,1},{9,5},{13,9},{1,13},{6,2},{10,6},{... | collective-permute-start | bytes 196616 | tf_op jit(solution)/shard_map/ppermute | solution.py:21
  184.1 6.1 %collective-permute-start.27 = (f32[1,64,256]{2,1,0:T(8,128)S(1)}, f32[1,64,256]{2,1,0:T(8,128)S(1)}, u32[]{:S(2)}, u32[]{:S(2)}) collective-permute-start(f32[1,64,256]{2,1,0:T(8,128)S(1)} %get-tuple-element.90), channel_id=1, source_target_pairs={{0,4},{4,8},{8,12},{12,0},{1,5},{5,9},{9,13},{13,1},{2,6},{6,10},{... | collective-permute-start | bytes 196616 | tf_op jit(solution)/shard_map/ppermute | solution.py:18
  191.4 4.9 %collective-permute-start.28 = (f32[1,64,256]{2,1,0:T(8,128)S(1)}, f32[1,64,256]{2,1,0:T(8,128)S(1)}, u32[]{:S(2)}, u32[]{:S(2)}) collective-permute-start(f32[1,64,256]{2,1,0:T(8,128)S(1)} %get-tuple-element.79), channel_id=1, source_target_pairs={{4,0},{8,4},{12,8},{0,12},{5,1},{9,5},{13,9},{1,13},{6,2},{10,6},{... | collective-permute-start | bytes 196616 | tf_op jit(solution)/shard_map/ppermute | solution.py:21
  191.5 6.8 %collective-permute-start.29 = (f32[1,64,256]{2,1,0:T(8,128)S(1)}, f32[1,64,256]{2,1,0:T(8,128)S(1)}, u32[]{:S(2)}, u32[]{:S(2)}) collective-permute-start(f32[1,64,256]{2,1,0:T(8,128)S(1)} %get-tuple-element.80), channel_id=1, source_target_pairs={{0,4},{4,8},{8,12},{12,0},{1,5},{5,9},{9,13},{13,1},{2,6},{6,10},{... | collective-permute-start | bytes 196616 | tf_op jit(solution)/shard_map/ppermute | solution.py:18
  200.7 6.1 %collective-permute-start.31 = (f32[1,64,256]{2,1,0:T(8,128)S(1)}, f32[1,64,256]{2,1,0:T(8,128)S(1)}, u32[]{:S(2)}, u32[]{:S(2)}) collective-permute-start(f32[1,64,256]{2,1,0:T(8,128)S(1)} %get-tuple-element.70), channel_id=1, source_target_pairs={{0,4},{4,8},{8,12},{12,0},{1,5},{5,9},{9,13},{13,1},{2,6},{6,10},{... | collective-permute-start | bytes 196616 | tf_op jit(solution)/shard_map/ppermute | solution.py:18
  217.3 6.3 %collective-permute-start.33 = (f32[1,64,256]{2,1,0:T(8,128)}, f32[1,64,256]{2,1,0:T(8,128)S(1)}, u32[]{:S(2)}, u32[]{:S(2)}) collective-permute-start(f32[1,64,256]{2,1,0:T(8,128)} %get-tuple-element.60), channel_id=1, source_target_pairs={{0,4},{4,8},{8,12},{12,0},{1,5},{5,9},{9,13},{13,1},{2,6},{6,10},{... | collective-permute-start | bytes 196616 | tf_op jit(solution)/shard_map/ppermute | solution.py:18
  (91 other events, 437.3 us)
Sparse Core Ops, SparseCore 0:
  217.4 20.6 reduce-scatter.1
where the time goes:
time: 246 us; the launch traced here: 245 us
  waiting for transfers between devices  116 us (47%)
  starting transfers between devices  36.5 us (15%)
  blocking collectives  30.7 us (12%)
  other arithmetic  26.8 us (11%)
  local copies, waits for them, and re-layouts  18.4 us (7%)
  between operations  15.6 us (6%)
    ppermute x17, waiting for transfers between devices, extended(): lax.ppermute(lax.slice_in_dim(block, 0, width, axis=dim), axis, backward)  55 us
    ppermute x17, waiting for transfers between devices, extended(): lax.ppermute(lax.slice_in_dim(block, block.shape[dim] - width, None, axis...  54.6 us
    psum x1, blocking collectives, on_device(): lax.psum(jnp.sum(probe * state), ('space', 'probe'))  30.7 us
    ppermute x17, starting transfers between devices, extended(): lax.ppermute(lax.slice_in_dim(block, block.shape[dim] - width, None, axis...  23.6 us
    ppermute x17, starting transfers between devices, extended(): lax.ppermute(lax.slice_in_dim(block, 0, width, axis=dim), axis, backward)  12.9 us
    broadcast_in_dim x1, other arithmetic, on_device(): return (costate[None], bond_grad)  8.26 us
    reduce_scatter x1, waiting for transfers between devices, on_device(): lax.psum_scatter(local_grad, 'probe', scatter_dimension=2, tiled=True)  6.27 us
    another operation x1, local copies, waits for them, and re-layouts, on_device(): jnp.stack([lax.psum(jnp.sum(probe * state), ('space', 'probe')) for state...  6.2 us
  transfers between devices with their start and end apart: 35, of which 35 were waited for; matrix products, arithmetic and copies ran while one was open for 5% of the time, Pallas kernels for 0%

commit v1 on v0

v1 whole, which is shorter than its diff:
```python
import functools

import jax
import jax.numpy as jnp
import numpy as np
from jax import lax
from jax.experimental import pallas as pl
from jax.experimental.pallas import tpu as pltpu
from jax.sharding import PartitionSpec as P

STEPS = 8
SCALE = 10.0
MESH = pl.DeviceIdType.MESH
ROWS = 16
LANES = 128


def tables(points):
    count = STEPS + 1
    order = np.arange(count)
    theta = np.pi * (np.arange(points) + 0.5) / points
    total = count + 1.0
    jackson = (
        (total - order) * np.cos(np.pi * order / total)
        + np.sin(np.pi * order / total) / np.tan(np.pi / total)
    ) / total
    table = np.zeros((ROWS, points), np.float32)
    table[:count] = np.cos(order[:, None] * theta[None, :])
    scaled = np.zeros((ROWS, LANES), np.float32)
    scaled[:count] = (np.where(order > 0, 2.0, 1.0) * jackson)[:, None]
    return table, scaled


def following(x, axis):
    return pltpu.roll(x, x.shape[axis] - 1, axis)


def preceding(x, axis):
    return pltpu.roll(x, 1, axis)


def flipped(index, bit):
    return index + bit - 2 * bit * lax.rem(lax.div(index, bit), 2)


def kernel(
    spaces, probes, total_sites,
    amp, mask, coup, target, table, scaled,
    costate, grad,
    v, du, q, g, bond, pair, low_product, high_mask, mom_a, mom_b, recv, direct,
    halo_send, halo_recv, edge_send, edge_recv,
    ma_send, ma_recv, mb_send, mb_recv, rs_send, rs_recv, d_send, d_recv,
):
    planes = mask.shape[0]
    last = planes - 1
    block = mask.shape[1] // probes
    s = lax.axis_index("space")
    p = lax.axis_index("probe")
    after, before = lax.rem(s + 1, spaces), lax.rem(s + spaces - 1, spaces)

    barrier = pltpu.get_barrier_semaphore()
    for off in range(1, spaces):
        pl.semaphore_signal(
            barrier, inc=1, device_id={"space": lax.rem(s + off, spaces)}, device_id_type=MESH
        )
    for off in range(1, probes):
        pl.semaphore_signal(
            barrier, inc=1, device_id={"probe": lax.rem(p + off, probes)}, device_id_type=MESH
        )

    started = []

    def send(src, dst, send_sem, recv_sem, where):
        copy = pltpu.make_async_remote_copy(
            src_ref=src, dst_ref=dst, send_sem=send_sem, recv_sem=recv_sem,
            device_id=where, device_id_type=MESH,
        )
        copy.start()
        started.append(copy)
        return copy

    for i in range(planes):
        v[0, i + 1] = amp[0, i] * mask[i]
    low_product[0] = (2.0 / SCALE) * (coup[0, last] * mask[last])
    pl.semaphore_wait(barrier, spaces + probes - 2)

    def send_low(k):
        return send(v.at[k, 1], v.at[k, planes + 1], halo_send.at[k, 0], halo_recv.at[k, 0], {"space": before})

    def send_high(k):
        return send(v.at[k, planes], v.at[k, 0], halo_send.at[k, 1], halo_recv.at[k, 1], {"space": after})

    edge_high = send(mask.at[0], high_mask.at[0], edge_send.at[0], edge_recv.at[0], {"space": before})
    edge_low = send(low_product.at[0], low_product.at[1], edge_send.at[1], edge_recv.at[1], {"space": after})
    from_high = send_low(0)
    from_low = send_high(0)

    for i in range(planes):
        m = mask[i]
        tenth = m * (1.0 / SCALE)
        if i < last:
            pair[0, i] = tenth * mask[i + 1]
            bond[0, i + 1] = 2.0 * coup[0, i] * pair[0, i]
        pair[1, i] = tenth * following(m, 0)
        pair[2, i] = tenth * following(m, 1)
        bond[1, i + 1] = 2.0 * coup[1, i] * pair[1, i]
        bond[2, i + 1] = 2.0 * coup[2, i] * pair[2, i]

    def moment(n, i, j):
        acc = v[i, 1] * v[j, 1]
        for plane in range(2, planes + 1):
            acc = acc + v[i, plane] * v[j, plane]
        row = jnp.sum(acc, axis=0, keepdims=True)
        part = row[:, :LANES]
        for start in range(LANES, row.shape[1], LANES):
            part = part + row[:, start:start + LANES]
        mom_a[p, pl.ds(n, 1), :] = part

    def product(n, d, i):
        acc = None
        for a in range(n // 2 + 1):
            term = du[d, a, i] * du[d, n - a, i]
            if a != n - a:
                term = 2.0 * term
            acc = term if acc is None else acc + term
        return acc

    def place(d, i):
        if d == 0:
            return 2 * planes + i
        return (d - 1) * planes + i

    sums = [None]

    def total_products(d, i, upto):
        acc = sums[0][1] * q[0, place(d, i)]
        for n in range(1, upto + 1):
            acc = acc + sums[0][n + 1] * q[n, place(d, i)]
        return acc

    mom_a[p, pl.ds(8, 8), :] = jnp.zeros((8, LANES), jnp.float32)
    a_copies, b_copies = [], []
    early = 3 * planes - 1
    rs_copies = {}
    weights = None

    def rows_of(index):
        return pl.ds(pl.multiple_of(index * block, block), block)

    def rs_start(level):
        bit = 1 << level
        other = flipped(p, bit)
        copies = []
        for j in range(probes // (2 * bit)):
            index = lax.rem(other, 2 * bit) + j * 2 * bit
            copies.append(send(
                g.at[pl.ds(0, early), rows_of(index)],
                recv.at[level, j],
                rs_send.at[level, j], rs_recv.at[level, j], {"probe": other},
            ))
        rs_copies[level] = copies

    def rs_finish(level):
        bit = 1 << level
        for j, copy in enumerate(rs_copies[level]):
            copy.wait_recv()
            index = lax.rem(p, 2 * bit) + j * 2 * bit
            g[pl.ds(0, early), rows_of(index)] = g[pl.ds(0, early), rows_of(index)] + recv[level, j]

    levels = probes.bit_length() - 1

    for k in range(STEPS):
        factor = 1.0 if k == 0 else 2.0
        across = [v[k, i + 1] - v[k, i + 2] for i in range(last)]
        for i in range(last):
            du[0, k, i] = factor * across[i]
        for i in range(planes):
            here = v[k, i + 1]
            d1 = here - following(here, 0)
            d2 = here - following(here, 1)
            du[1, k, i] = factor * d1
            du[2, k, i] = factor * d2
            f1 = bond[1, i + 1] * d1
            f2 = bond[2, i + 1] * d2
            inside = (f1 - preceding(f1, 0)) + (f2 - preceding(f2, 1))
            if i < last:
                inside = inside + bond[0, i + 1] * across[i]
            if i > 0:
                inside = inside - bond[0, i] * across[i - 1]
            if k == 0:
                v[1, i + 1] = 0.5 * inside - here
            else:
                v[k + 1, i + 1] = inside - 2.0 * here - v[k - 1, i + 1]

        if k <= 4:
            if k == 0:
                moment(0, 0, 0)
            else:
                moment(2 * k - 1, k - 1, k)
                moment(2 * k, k, k)
        if k == 4:
            for off in range(1, probes):
                a_copies.append(send(
                    mom_a.at[p], mom_a.at[p], ma_send.at[off], ma_recv.at[off],
                    {"probe": lax.rem(p + off, probes)},
                ))
        if k == 5:
            for copy in a_copies:
                copy.wait_recv()
            acc = mom_a[0]
            for index in range(1, probes):
                acc = acc + mom_a[index]
            mom_b[s] = acc
            for off in range(1, spaces):
                b_copies.append(send(
                    mom_b.at[s], mom_b.at[s], mb_send.at[off], mb_recv.at[off],
                    {"space": lax.rem(s + off, spaces)},
                ))
        if k == 6:
            for copy in b_copies:
                copy.wait_recv()
            acc = mom_b[0]
            for index in range(1, spaces):
                acc = acc + mom_b[index]
            raw = jnp.sum(acc, axis=1, keepdims=True) / total_sites
            base0, base1 = raw[0:1], raw[1:2]
            moments = [base0, base1]
            for n in range(2, STEPS + 1):
                moments.append(2.0 * raw[n:n + 1] - (base0 if n % 2 == 0 else base1))
            points = target.shape[1]
            spectrum = jnp.zeros((1, points), jnp.float32)
            for n in range(STEPS + 1):
                spectrum = spectrum + scaled[n:n + 1, 0:1] * moments[n] * table[n:n + 1, :]
            misfit = spectrum - target[...]
            weights = []
            for n in range(STEPS + 1):
                dot = jnp.sum(table[n:n + 1, :] * misfit, axis=1, keepdims=True)
                weights.append((2.0 / points) * scaled[n:n + 1, 0:1] * dot)
            partial = [None] * (STEPS + 1)
            for n in range(STEPS, 0, -1):
                partial[n] = weights[n] if n + 2 > STEPS else weights[n] + partial[n + 2]
            sums[0] = partial

        for d, i in [(d, i) for d in (1, 2, 0) for i in range(planes)]:
            if d == 0 and i == last:
                continue
            if k < STEPS - 1:
                q[k, place(d, i)] = product(k, d, i)
            else:
                whole = total_products(d, i, k - 1) + sums[0][k + 1] * product(k, d, i)
                g[place(d, i)] = pair[d, i] * whole
        if k == STEPS - 1:
            rs_start(0)
            for i in range(planes):
                acc = weights[0] * v[0, i + 1]
                for n in range(1, STEPS):
                    acc = acc + weights[n] * v[n, i + 1]
                costate[0, i] = 2.0 * acc
            for level in range(levels):
                rs_finish(level)
                if level + 1 < levels:
                    rs_start(level + 1)

        if k == 0:
            edge_high.wait_recv()
            pair[0, last] = mask[last] * (1.0 / SCALE) * high_mask[0]
            bond[0, planes] = 2.0 * coup[0, last] * pair[0, last]
            edge_low.wait_recv()
            bond[0, 0] = low_product[1] * mask[0]
        share = 0.5 if k == 0 else 1.0
        from_high.wait_recv()
        top = v[k, planes] - v[k, planes + 1]
        v[k + 1, planes] = v[k + 1, planes] + share * bond[0, planes] * top
        if k + 1 < STEPS:
            next_low = send_high(k + 1)
        du[0, k, last] = factor * top
        from_low.wait_recv()
        bottom = v[k, 0] - v[k, 1]
        v[k + 1, 1] = v[k + 1, 1] - share * bond[0, 0] * bottom
        if k + 1 < STEPS:
            next_high = send_low(k + 1)
            from_high, from_low = next_high, next_low
            q[k, place(0, last)] = product(k, 0, last)

    k = STEPS - 1
    whole = total_products(0, last, k - 1) + sums[0][k + 1] * product(k, 0, last)
    g[early] = pair[0, last] * whole
    d_copies = []
    for off in range(1, probes):
        other = lax.rem(p + off, probes)
        d_copies.append(send(
            g.at[early, rows_of(other)], direct.at[off - 1], d_send.at[off], d_recv.at[off],
            {"probe": other},
        ))
    for i in range(planes):
        costate[0, i] = costate[0, i] + 2.0 * weights[STEPS] * v[STEPS, i + 1]
    for d, i in [(d, i) for d in (1, 2, 0) for i in range(planes)]:
        if d == 0 and i == last:
            continue
        grad[d, i] = g[place(d, i), rows_of(p)]
    acc = g[early, rows_of(p)]
    for off in range(1, probes):
        d_copies[off - 1].wait_recv()
        acc = acc + direct[off - 1]
    grad[0, last] = acc
    for copy in started:
        copy.wait_send()


def on_device(probe_amplitudes, site_mask, couplings, target):
    spaces, probes = lax.axis_size("space"), lax.axis_size("probe")
    planes, rows, lanes = site_mask.shape
    table, scaled = tables(target.shape[0])
    block = rows // probes
    levels = probes.bit_length() - 1
    f32 = jnp.float32
    total_sites = float(probes * spaces * planes * rows * lanes)
    vmem = pl.BlockSpec(memory_space=pltpu.VMEM)
    dma = pltpu.SemaphoreType.DMA
    return pl.pallas_call(
        functools.partial(kernel, spaces, probes, total_sites),
        out_shape=(
            jax.ShapeDtypeStruct((1, planes, rows, lanes), f32),
            jax.ShapeDtypeStruct((3, planes, block, lanes), f32),
        ),
        in_specs=[vmem] * 6,
        out_specs=(vmem, vmem),
        scratch_shapes=[
            pltpu.VMEM((STEPS + 1, planes + 2, rows, lanes), f32),
            pltpu.VMEM((3, STEPS, planes, rows, lanes), f32),
            pltpu.VMEM((STEPS, 3 * planes, rows, lanes), f32),
            pltpu.VMEM((3 * planes, rows, lanes), f32),
            pltpu.VMEM((3, planes + 1, rows, lanes), f32),
            pltpu.VMEM((3, planes, rows, lanes), f32),
            pltpu.VMEM((2, rows, lanes), f32),
            pltpu.VMEM((1, rows, lanes), f32),
            pltpu.VMEM((probes, ROWS, LANES), f32),
            pltpu.VMEM((spaces, ROWS, LANES), f32),
            pltpu.VMEM((levels, probes // 2, 3 * planes - 1, block, lanes), f32),
            pltpu.VMEM((probes - 1, block, lanes), f32),
            dma((STEPS, 2)), dma((STEPS, 2)), dma((2,)), dma((2,)),
            dma((probes,)), dma((probes,)), dma((spaces,)), dma((spaces,)),
            dma((levels, probes // 2)), dma((levels, probes // 2)),
            dma((probes,)), dma((probes,)),
        ],
        compiler_params=pltpu.CompilerParams(
            collective_id=0, has_side_effects=True, vmem_limit_bytes=48 * 1024 * 1024
        ),
    )(probe_amplitudes, site_mask, couplings, target[None], table, scaled)


def solution(mesh):
    return jax.shard_map(
        on_device,
        mesh=mesh,
        in_specs=(
            P(("groups", "probe"), "space", None, None),
            P(("groups", "space"), None, None),
            P(None, ("groups", "space"), None, None),
            P("groups"),
        ),
        out_specs=(
            P(("groups", "probe"), "space", None, None),
            P(None, ("groups", "space"), "probe", None),
        ),
        check_vma=False,
    )
```

time: 246 us -> 57.9 us (0.24)
  waiting for transfers between devices: 116 us -> 0 us
  Pallas kernels: 0 us -> 50.6 us
  starting transfers between devices: 36.5 us -> 0 us
  blocking collectives: 30.7 us -> 0 us
  other arithmetic: 26.8 us -> 0 us
  between operations: 15.6 us -> 0.65 us
  local copies, waits for them, and re-layouts: 18.4 us -> 6.34 us
    ppermute x34 -> x0, waiting for transfers between devices: 110 us -> none  [the longest x17 55 us: extended(): lax.ppermute(lax.slice_in_dim(block, 0, width, axis=dim), axis, backward)]
    pallas_call x0 -> x1, Pallas kernels: none -> 50.6 us  [on_device(): pl.pallas_call(functools.partial(kernel, spaces, probes, total_sites), ou...]
    ppermute x34 -> x0, starting transfers between devices: 36.5 us -> none  [the longest x17 23.6 us: extended(): lax.ppermute(lax.slice_in_dim(block, block.shape[dim] - width, None, axis...]
    psum x1 -> x0, blocking collectives: 30.7 us -> none  [on_device(): lax.psum(jnp.sum(probe * state), ('space', 'probe'))]
    slice x94 -> x0, local copies, waits for them, and re-layouts: 8.57 us -> none  [the longest x64 5.66 us: apply_field(): jnp.roll(centre, -1, axis)]
    broadcast_in_dim x1 -> x0, other arithmetic: 8.26 us -> none  [on_device(): return (costate[None], bond_grad)]
    sub x14 -> x0, other arithmetic: 7.84 us -> none  [the longest x6 6.13 us: on_device(): earlier = weights[step - 1] * probe + 2.0 * image - beyond]
    reduce_scatter x1 -> x0, waiting for transfers between devices: 6.27 us -> none  [on_device(): lax.psum_scatter(local_grad, 'probe', scatter_dimension=2, tiled=True)]
  transfers between devices with their start and end apart: 35 -> 0, of which waited for: 35 -> 0; matrix products, arithmetic and copies ran while one was open for 5% -> 0% of each run, Pallas kernels for 0% -> 0%
where the time goes in v1:
time: 57.9 us; the launch traced here: 57.6 us
  Pallas kernels  50.6 us (87%)
  local copies, waits for them, and re-layouts  6.34 us (11%)
  between operations  0.65 us (1%)
    pallas_call x1, Pallas kernels, on_device(): pl.pallas_call(functools.partial(kernel, spaces, probes, total_sites), ou...  50.6 us
    unnamed x14, local copies, waits for them, and re-layouts  6.34 us

profile of v1, /device:TPU:0, one launch (start us, length us, event | category | flops | bytes accessed | tf_op | source)
XLA Modules:
  0.0 57.6 jit_solution(15230850250094787456)
XLA Ops:
  0.6 0.0 copy-start.5
  0.6 0.7 %copy-done.5 = f32[256]{0:T(256)S(1)} copy-done((f32[256]{0:T(256)S(1)}, f32[256]{0:T(256)}, u32[]{:S(2)}) %copy-start.5) | copy-done | bytes 1048
  1.3 0.0 copy-start
  1.3 1.1 %copy-done = f32[3,3,64,256]{3,2,1,0:T(8,128)S(1)} copy-done((f32[3,3,64,256]{3,2,1,0:T(8,128)S(1)}, f32[3,3,64,256]{3,2,1,0:T(8,128)}, u32[]{:S(2)}) %copy-start) | copy-done | bytes 589848
  2.4 0.0 copy-start.1
  2.4 0.9 %copy-done.1 = f32[1,3,64,256]{3,2,1,0:T(8,128)S(1)} copy-done((f32[1,3,64,256]{3,2,1,0:T(8,128)S(1)}, f32[1,3,64,256]{3,2,1,0:T(8,128)}, u32[]{:S(2)}) %copy-start.1) | copy-done | bytes 196632
  3.3 0.0 copy-start.2
  3.3 0.9 %copy-done.2 = f32[3,64,256]{2,1,0:T(8,128)S(1)} copy-done((f32[3,64,256]{2,1,0:T(8,128)S(1)}, f32[3,64,256]{2,1,0:T(8,128)}, u32[]{:S(2)}) %copy-start.2) | copy-done | bytes 196632
  4.2 0.0 copy-start.3
  4.2 0.7 %copy-done.3 = f32[16,256]{1,0:T(8,128)S(1)} copy-done((f32[16,256]{1,0:T(8,128)S(1)}, f32[16,256]{1,0:T(8,128)}, u32[]{:S(2)}) %copy-start.3) | copy-done | bytes 16408
  4.9 0.0 copy-start.4
  5.0 0.7 %copy-done.4 = f32[16,128]{1,0:T(8,128)S(1)} copy-done((f32[16,128]{1,0:T(8,128)S(1)}, f32[16,128]{1,0:T(8,128)}, u32[]{:S(2)}) %copy-start.4) | copy-done | bytes 8216
  5.6 50.6 %shard_map.77 = (f32[1,3,64,256]{3,2,1,0:T(8,128)S(1)}, f32[3,3,16,256]{3,2,1,0:T(8,128)S(1)}) custom-call(f32[1,3,64,256]{3,2,1,0:T(8,128)S(1)} %copy-done.1, f32[3,64,256]{2,1,0:T(8,128)S(1)} %copy-done.2, f32[3,3,64,256]{3,2,1,0:T(8,128)S(1)} %copy-done, f32[1,256]{1,0:T(1,128)S(1)} %bitcast.1, f32[16,256]{1,0:T(8,128)S(1)} %copy-done.3, ...), custom_call_target="tpu_custom_call" | custom-call | tf_op jit(solution)/shard_map/pallas_call | solution.py:320
  56.2 0.7 %copy.10 = f32[1,3,64,256]{3,2,1,0:T(8,128)} copy(f32[1,3,64,256]{3,2,1,0:T(8,128)S(1)} %get-tuple-element.4) | data formatting | bytes 393216
  56.9 0.7 %copy.11 = f32[3,3,16,256]{3,2,1,0:T(8,128)} copy(f32[3,3,16,256]{3,2,1,0:T(8,128)S(1)} %get-tuple-element.5) | data formatting | bytes 294912
Async XLA Ops:
  0.6 0.7 %copy-start.5 = (f32[256]{0:T(256)S(1)}, f32[256]{0:T(256)}, u32[]{:S(2)}) copy-start(f32[256]{0:T(256)} %param.9) | copy-start | bytes 3076
  1.3 1.1 %copy-start = (f32[3,3,64,256]{3,2,1,0:T(8,128)S(1)}, f32[3,3,64,256]{3,2,1,0:T(8,128)}, u32[]{:S(2)}) copy-start(f32[3,3,64,256]{3,2,1,0:T(8,128)} %coup.1) | copy-start | bytes 1769476
  2.4 0.9 %copy-start.1 = (f32[1,3,64,256]{3,2,1,0:T(8,128)S(1)}, f32[1,3,64,256]{3,2,1,0:T(8,128)}, u32[]{:S(2)}) copy-start(f32[1,3,64,256]{3,2,1,0:T(8,128)} %amp.1) | copy-start | bytes 589828
  3.3 0.9 %copy-start.2 = (f32[3,64,256]{2,1,0:T(8,128)S(1)}, f32[3,64,256]{2,1,0:T(8,128)}, u32[]{:S(2)}) copy-start(f32[3,64,256]{2,1,0:T(8,128)} %mask.1) | copy-start | bytes 589828
  4.2 0.7 %copy-start.3 = (f32[16,256]{1,0:T(8,128)S(1)}, f32[16,256]{1,0:T(8,128)}, u32[]{:S(2)}) copy-start(f32[16,256]{1,0:T(8,128)} %constant.4.clone.table) | copy-start | bytes 49156
  4.9 0.7 %copy-start.4 = (f32[16,128]{1,0:T(8,128)S(1)}, f32[16,128]{1,0:T(8,128)}, u32[]{:S(2)}) copy-start(f32[16,128]{1,0:T(8,128)} %constant.5.clone.scaled) | copy-start | bytes 24580

commit v2 on v1

v2 whole, which is shorter than its diff:
```python
import functools

import jax
import jax.numpy as jnp
import numpy as np
from jax import lax
from jax.experimental import pallas as pl
from jax.experimental.pallas import tpu as pltpu
from jax.sharding import PartitionSpec as P

STEPS = 8
SCALE = 10.0
MESH = pl.DeviceIdType.MESH
ROWS = 16
LANES = 128


def tables(points):
    count = STEPS + 1
    order = np.arange(count)
    theta = np.pi * (np.arange(points) + 0.5) / points
    total = count + 1.0
    jackson = (
        (total - order) * np.cos(np.pi * order / total)
        + np.sin(np.pi * order / total) / np.tan(np.pi / total)
    ) / total
    table = np.zeros((ROWS, points), np.float32)
    table[:count] = np.cos(order[:, None] * theta[None, :])
    scaled = np.zeros((ROWS, LANES), np.float32)
    scaled[:count] = (np.where(order > 0, 2.0, 1.0) * jackson)[:, None]
    return table, scaled


def following(x, axis):
    return pltpu.roll(x, x.shape[axis] - 1, axis)


def preceding(x, axis):
    return pltpu.roll(x, 1, axis)


def flipped(index, bit):
    return index + bit - 2 * bit * lax.rem(lax.div(index, bit), 2)


def kernel(
    spaces, probes, total_sites,
    amp_in, mask_in, coup_in, target_in, table_in, scaled_in,
    costate, grad,
    amp, mask, coup, target, table, scaled,
    v, du, q, g, bond, pair, give, got, mom_a, mom_b, recv, direct,
    load_sem, edge_send, edge_recv, mid_send, mid_recv,
    give_send, give_recv, pass_send, pass_recv,
    ma_send, ma_recv, mb_send, mb_recv, rs_send, rs_recv, d_send, d_recv,
):
    planes, rows, _ = mask.shape
    first, last, high = 2, planes + 1, planes + 2
    middle = 3
    block = rows // probes
    half = rows // 2
    s = lax.axis_index("space")
    p = lax.axis_index("probe")
    after, before = lax.rem(s + 1, spaces), lax.rem(s + spaces - 1, spaces)
    twin = flipped(p, 1)

    loads = []
    for n, (src, dst) in enumerate([
        (mask_in, mask), (amp_in, amp), (coup_in, coup),
        (target_in, target), (table_in, table), (scaled_in, scaled),
    ]):
        loads.append(pltpu.make_async_copy(src, dst, load_sem.at[n]))
        loads[-1].start()
    barrier = pltpu.get_barrier_semaphore()
    for off in range(1, spaces):
        pl.semaphore_signal(
            barrier, inc=1, device_id={"space": lax.rem(s + off, spaces)}, device_id_type=MESH
        )
    for off in range(1, probes):
        pl.semaphore_signal(
            barrier, inc=1, device_id={"probe": lax.rem(p + off, probes)}, device_id_type=MESH
        )

    started = []

    def send(src, dst, send_sem, recv_sem, where):
        copy = pltpu.make_async_remote_copy(
            src_ref=src, dst_ref=dst, send_sem=send_sem, recv_sem=recv_sem,
            device_id=where, device_id_type=MESH,
        )
        copy.start()
        started.append(copy)
        return copy

    low_mid, high_mid = {}, {}

    def send_middle(k):
        low_mid[k] = send(
            v.at[k, middle], v.at[k, 0], mid_send.at[k, 0], mid_recv.at[k, 0], {"space": after}
        )
        high_mid[k] = send(
            v.at[k, middle], v.at[k, high + 1], mid_send.at[k, 1], mid_recv.at[k, 1], {"space": before}
        )

    own_half = pl.ds(pl.multiple_of(lax.rem(p, 2) * half, half), half)

    def send_bonds(group, start, size):
        out = []
        for side, where in ((0, after), (1, before)):
            out.append(send(
                give.at[side, pl.ds(start, size), own_half],
                got.at[side, pl.ds(start, size), own_half],
                give_send.at[group, side], give_recv.at[group, side], {"space": where},
            ))
        return out

    def pass_bonds(group, start, size, copies):
        out = []
        for side in (0, 1):
            copies[side].wait_recv()
            out.append(send(
                got.at[side, pl.ds(start, size), own_half],
                got.at[side, pl.ds(start, size), own_half],
                pass_send.at[group, side], pass_recv.at[group, side], {"probe": twin},
            ))
        return out

    for n in (0, 1):
        loads[n].wait()
    for i in range(planes):
        v[0, first + i] = amp[0, i] * mask[i]
    pl.semaphore_wait(barrier, spaces + probes - 2)
    edge_low = send(v.at[0, last], v.at[0, 1], edge_send.at[0], edge_recv.at[0], {"space": after})
    edge_high = send(v.at[0, first], v.at[0, high], edge_send.at[1], edge_recv.at[1], {"space": before})
    loads[2].wait()
    give[0, 0] = (2.0 / SCALE) * (coup[0, planes - 1] * mask[planes - 1])
    give[1, 0] = mask[0]
    near = send_bonds(0, 0, 1)
    send_middle(0)

    for i in range(planes):
        m = mask[i]
        tenth = m * (1.0 / SCALE)
        if i < planes - 1:
            pair[0, i] = tenth * mask[i + 1]
            bond[0, first + i] = 2.0 * coup[0, i] * pair[0, i]
        pair[1, i] = tenth * following(m, 0)
        pair[2, i] = tenth * following(m, 1)
        for d in (1, 2):
            bond[d, first + i] = 2.0 * coup[d, i] * pair[d, i]
    give[0, 1] = bond[0, last - 1]
    give[1, 1] = bond[0, first]
    for d in (1, 2):
        give[0, d + 1] = bond[d, last]
        give[1, d + 1] = bond[d, first]
    far = send_bonds(1, 1, 3)

    def strength(d, j):
        if d == 0 and j == 0:
            return got[0, 1]
        if d == 0 and j == high:
            return got[1, 1]
        if d > 0 and j == 1:
            return got[0, d + 1]
        if d > 0 and j == high:
            return got[1, d + 1]
        return bond[d, j]

    def factor(k):
        return 1.0 if k == 0 else 2.0

    def step(k, j):
        here = v[k, j]
        d0 = here - v[k, j + 1]
        d1 = here - following(here, 0)
        d2 = here - following(here, 1)
        f1 = strength(1, j) * d1
        f2 = strength(2, j) * d2
        inside = (f1 - preceding(f1, 0)) + (f2 - preceding(f2, 1))
        inside = inside + strength(0, j) * d0
        inside = inside + strength(0, j - 1) * (here - v[k, j - 1])
        if k == 0:
            v[1, j] = 0.5 * inside - here
        else:
            v[k + 1, j] = inside - 2.0 * here - v[k - 1, j]
        if first <= j <= last and k < STEPS - 1:
            du[0, k, j - first] = factor(k) * d0
            du[1, k, j - first] = factor(k) * d1
            du[2, k, j - first] = factor(k) * d2

    def moment(n, i, j):
        acc = v[i, first] * v[j, first]
        for plane in range(first + 1, last + 1):
            acc = acc + v[i, plane] * v[j, plane]
        row = jnp.sum(acc, axis=0, keepdims=True)
        part = row[:, :LANES]
        for start in range(LANES, row.shape[1], LANES):
            part = part + row[:, start:start + LANES]
        mom_a[p, pl.ds(n, 1), :] = part

    def product(n, d, i):
        acc = None
        for a in range(n // 2 + 1):
            term = du[d, a, i] * du[d, n - a, i]
            if a != n - a:
                term = 2.0 * term
            acc = term if acc is None else acc + term
        return acc

    def place(d, i):
        if d == 0:
            return 2 * planes + i
        return (d - 1) * planes + i

    every = [(d, i) for d in (1, 2, 0) for i in range(planes)]
    early = 3 * planes - 1

    def products(n):
        for d, i in every:
            q[n, place(d, i)] = product(n, d, i)

    def gradient(d, i, sums):
        acc = sums[STEPS] * product(STEPS - 1, d, i)
        for n in range(STEPS - 1):
            acc = acc + sums[n + 1] * q[n, place(d, i)]
        g[place(d, i)] = pair[d, i] * acc

    def rows_of(index):
        return pl.ds(pl.multiple_of(index * block, block), block)

    levels = probes.bit_length() - 1
    rs_copies = {}

    def rs_start(level):
        bit = 1 << level
        other = flipped(p, bit)
        rs_copies[level] = []
        for j in range(probes // (2 * bit)):
            index = lax.rem(other, 2 * bit) + j * 2 * bit
            rs_copies[level].append(send(
                g.at[pl.ds(0, early), rows_of(index)], recv.at[level, j],
                rs_send.at[level, j], rs_recv.at[level, j], {"probe": other},
            ))

    def rs_finish(level):
        bit = 1 << level
        for j, copy in enumerate(rs_copies[level]):
            copy.wait_recv()
            index = lax.rem(p, 2 * bit) + j * 2 * bit
            g[pl.ds(0, early), rows_of(index)] = g[pl.ds(0, early), rows_of(index)] + recv[level, j]

    step(0, middle)
    send_middle(1)
    near = pass_bonds(0, 0, 1, near)
    mom_a[p, pl.ds(8, 8), :] = jnp.zeros((8, LANES), jnp.float32)
    moment(0, 0, 0)
    for copy in near:
        copy.wait_recv()
    bond[0, 1] = got[0, 0] * mask[0]
    pair[0, planes - 1] = mask[planes - 1] * (1.0 / SCALE) * got[1, 0]
    bond[0, last] = 2.0 * coup[0, planes - 1] * pair[0, planes - 1]
    edge_low.wait_recv()
    step(0, first)
    edge_high.wait_recv()
    step(0, last)
    step(1, middle)
    send_middle(2)
    far = pass_bonds(1, 1, 3, far)
    moment(1, 0, 1)
    moment(2, 1, 1)
    products(0)
    for copy in far:
        copy.wait_recv()

    a_copies, b_copies = [], []
    weights, sums = None, None
    for t in range(STEPS - 1):
        low_mid[t].wait_recv()
        step(t, 1)
        step(t + 1, first)
        high_mid[t].wait_recv()
        step(t, high)
        step(t + 1, last)
        if t + 2 < STEPS:
            step(t + 2, middle)
        if t + 3 < STEPS - 1:
            send_middle(t + 3)

        if t < 3:
            moment(2 * t + 3, t + 1, t + 2)
            moment(2 * t + 4, t + 2, t + 2)
        if t == 2:
            for off in range(1, probes):
                a_copies.append(send(
                    mom_a.at[p], mom_a.at[p], ma_send.at[off], ma_recv.at[off],
                    {"probe": lax.rem(p + off, probes)},
                ))
        if t == 3:
            for copy in a_copies:
                copy.wait_recv()
            acc = mom_a[0]
            for index in range(1, probes):
                acc = acc + mom_a[index]
            mom_b[s] = acc
            for off in range(1, spaces):
                b_copies.append(send(
                    mom_b.at[s], mom_b.at[s], mb_send.at[off], mb_recv.at[off],
                    {"space": lax.rem(s + off, spaces)},
                ))
        if t < STEPS - 2:
            products(t + 1)
        if t == STEPS - 3:
            for n in (3, 4, 5):
                loads[n].wait()
            for copy in b_copies:
                copy.wait_recv()
            acc = mom_b[0]
            for index in range(1, spaces):
                acc = acc + mom_b[index]
            raw = jnp.sum(acc, axis=1, keepdims=True) / total_sites
            base = (raw[0:1], raw[1:2])
            moments = list(base)
            for n in range(2, STEPS + 1):
                moments.append(2.0 * raw[n:n + 1] - base[n % 2])
            points = target.shape[1]
            spectrum = jnp.zeros((1, points), jnp.float32)
            for n in range(STEPS + 1):
                spectrum = spectrum + scaled[n:n + 1, 0:1] * moments[n] * table[n:n + 1, :]
            misfit = spectrum - target[...]
            weights = []
            for n in range(STEPS + 1):
                dot = jnp.sum(table[n:n + 1, :] * misfit, axis=1, keepdims=True)
                weights.append((2.0 / points) * scaled[n:n + 1, 0:1] * dot)
            sums = [None] * (STEPS + 1)
            for n in range(STEPS, 0, -1):
                sums[n] = weights[n] if n + 2 > STEPS else weights[n] + sums[n + 2]
            k = STEPS - 1
            for i in range(planes):
                here = v[k, first + i]
                du[1, k, i] = 2.0 * (here - following(here, 0))
                du[2, k, i] = 2.0 * (here - following(here, 1))
                if i < planes - 1:
                    du[0, k, i] = 2.0 * (here - v[k, first + i + 1])
            for d, i in every[:-1]:
                gradient(d, i, sums)
            rs_start(0)
            for i in range(planes):
                acc = weights[0] * v[0, first + i]
                for n in range(1, STEPS):
                    acc = acc + weights[n] * v[n, first + i]
                costate[0, i] = 2.0 * acc
            rs_finish(0)
            if levels > 1:
                rs_start(1)

    k = STEPS - 1
    du[0, k, planes - 1] = 2.0 * (v[k, last] - v[k, high])
    gradient(0, planes - 1, sums)
    d_copies = []
    for off in range(1, probes):
        other = lax.rem(p + off, probes)
        d_copies.append(send(
            g.at[early, rows_of(other)], direct.at[off - 1], d_send.at[off], d_recv.at[off],
            {"probe": other},
        ))
    for i in range(planes):
        costate[0, i] = costate[0, i] + 2.0 * weights[STEPS] * v[STEPS, first + i]
    for level in range(1, levels):
        rs_finish(level)
        if level + 1 < levels:
            rs_start(level + 1)
    for d, i in every[:-1]:
        grad[d, i] = g[place(d, i), rows_of(p)]
    acc = g[early, rows_of(p)]
    for off in range(1, probes):
        d_copies[off - 1].wait_recv()
        acc = acc + direct[off - 1]
    grad[0, planes - 1] = acc
    for copy in started:
        copy.wait_send()


def on_device(probe_amplitudes, site_mask, couplings, target):
    spaces, probes = lax.axis_size("space"), lax.axis_size("probe")
    planes, rows, lanes = site_mask.shape
    table, scaled = tables(target.shape[0])
    block = rows // probes
    levels = probes.bit_length() - 1
    f32 = jnp.float32
    total_sites = float(probes * spaces * planes * rows * lanes)
    vmem = pl.BlockSpec(memory_space=pltpu.VMEM)
    dma = pltpu.SemaphoreType.DMA
    return pl.pallas_call(
        functools.partial(kernel, spaces, probes, total_sites),
        out_shape=(
            jax.ShapeDtypeStruct((1, planes, rows, lanes), f32),
            jax.ShapeDtypeStruct((3, planes, block, lanes), f32),
        ),
        in_specs=[pl.BlockSpec(memory_space=pl.ANY)] * 6,
        out_specs=(vmem, vmem),
        scratch_shapes=[
            pltpu.VMEM(probe_amplitudes.shape, f32),
            pltpu.VMEM(site_mask.shape, f32),
            pltpu.VMEM(couplings.shape, f32),
            pltpu.VMEM((1, target.shape[0]), f32),
            pltpu.VMEM(table.shape, f32),
            pltpu.VMEM(scaled.shape, f32),
            pltpu.VMEM((STEPS + 1, planes + 4, rows, lanes), f32),
            pltpu.VMEM((3, STEPS, planes, rows, lanes), f32),
            pltpu.VMEM((STEPS, 3 * planes, rows, lanes), f32),
            pltpu.VMEM((3 * planes, rows, lanes), f32),
            pltpu.VMEM((3, planes + 3, rows, lanes), f32),
            pltpu.VMEM((3, planes, rows, lanes), f32),
            pltpu.VMEM((2, 4, rows, lanes), f32),
            pltpu.VMEM((2, 4, rows, lanes), f32),
            pltpu.VMEM((probes, ROWS, LANES), f32),
            pltpu.VMEM((spaces, ROWS, LANES), f32),
            pltpu.VMEM((levels, probes // 2, 3 * planes - 1, block, lanes), f32),
            pltpu.VMEM((probes - 1, block, lanes), f32),
            dma((6,)), dma((2,)), dma((2,)), dma((STEPS, 2)), dma((STEPS, 2)),
            dma((2, 2)), dma((2, 2)), dma((2, 2)), dma((2, 2)),
            dma((probes,)), dma((probes,)), dma((spaces,)), dma((spaces,)),
            dma((levels, probes // 2)), dma((levels, probes // 2)),
            dma((probes,)), dma((probes,)),
        ],
        compiler_params=pltpu.CompilerParams(
            collective_id=0, has_side_effects=True, vmem_limit_bytes=48 * 1024 * 1024
        ),
    )(probe_amplitudes, site_mask, couplings, target[None], table, scaled)


def solution(mesh):
    return jax.shard_map(
        on_device,
        mesh=mesh,
        in_specs=(
            P(("groups", "probe"), "space", None, None),
            P(("groups", "space"), None, None),
            P(None, ("groups", "space"), None, None),
            P("groups"),
        ),
        out_specs=(
            P(("groups", "probe"), "space", None, None),
            P(None, ("groups", "space"), "probe", None),
        ),
        check_vma=False,
    )
```

time: 57.9 us -> 52.3 us (0.903)
  Pallas kernels: 50.6 us -> 45 us
    pallas_call x1, Pallas kernels: 50.6 us -> 45 us  [on_device(): pl.pallas_call(functools.partial(kernel, spaces, probes, total_sites), ou...]
where the time goes in v2:
time: 52.3 us; the launch traced here: 52 us
  Pallas kernels  45 us (86%)
  local copies, waits for them, and re-layouts  6.34 us (12%)
  between operations  0.65 us (1%)
    pallas_call x1, Pallas kernels, on_device(): pl.pallas_call(functools.partial(kernel, spaces, probes, total_sites), ou...  45 us
    unnamed x14, local copies, waits for them, and re-layouts  6.34 us

profile of v2, /device:TPU:0, one launch (start us, length us, event | category | flops | bytes accessed | tf_op | source)
XLA Modules:
  0.0 52.0 jit_solution(9101850064695753473)
XLA Ops:
  0.6 0.0 copy-start.5
  0.6 0.7 %copy-done.5 = f32[256]{0:T(256)S(1)} copy-done((f32[256]{0:T(256)S(1)}, f32[256]{0:T(256)}, u32[]{:S(2)}) %copy-start.5) | copy-done | bytes 1048
  1.3 0.0 copy-start
  1.3 1.1 %copy-done = f32[3,3,64,256]{3,2,1,0:T(8,128)S(1)} copy-done((f32[3,3,64,256]{3,2,1,0:T(8,128)S(1)}, f32[3,3,64,256]{3,2,1,0:T(8,128)}, u32[]{:S(2)}) %copy-start) | copy-done | bytes 589848
  2.4 0.0 copy-start.1
  2.4 0.9 %copy-done.1 = f32[1,3,64,256]{3,2,1,0:T(8,128)S(1)} copy-done((f32[1,3,64,256]{3,2,1,0:T(8,128)S(1)}, f32[1,3,64,256]{3,2,1,0:T(8,128)}, u32[]{:S(2)}) %copy-start.1) | copy-done | bytes 196632
  3.3 0.0 copy-start.2
  3.3 0.9 %copy-done.2 = f32[3,64,256]{2,1,0:T(8,128)S(1)} copy-done((f32[3,64,256]{2,1,0:T(8,128)S(1)}, f32[3,64,256]{2,1,0:T(8,128)}, u32[]{:S(2)}) %copy-start.2) | copy-done | bytes 196632
  4.2 0.0 copy-start.3
  4.2 0.7 %copy-done.3 = f32[16,256]{1,0:T(8,128)S(1)} copy-done((f32[16,256]{1,0:T(8,128)S(1)}, f32[16,256]{1,0:T(8,128)}, u32[]{:S(2)}) %copy-start.3) | copy-done | bytes 16408
  4.9 0.0 copy-start.4
  5.0 0.7 %copy-done.4 = f32[16,128]{1,0:T(8,128)S(1)} copy-done((f32[16,128]{1,0:T(8,128)S(1)}, f32[16,128]{1,0:T(8,128)}, u32[]{:S(2)}) %copy-start.4) | copy-done | bytes 8216
  5.6 45.0 %shard_map.77 = (f32[1,3,64,256]{3,2,1,0:T(8,128)S(1)}, f32[3,3,16,256]{3,2,1,0:T(8,128)S(1)}) custom-call(f32[1,3,64,256]{3,2,1,0:T(8,128)S(1)} %copy-done.1, f32[3,64,256]{2,1,0:T(8,128)S(1)} %copy-done.2, f32[3,3,64,256]{3,2,1,0:T(8,128)S(1)} %copy-done, f32[1,256]{1,0:T(1,128)S(1)} %bitcast.1, f32[16,256]{1,0:T(8,128)S(1)} %copy-done.3, ...), custom_call_target="tpu_custom_call" | custom-call | tf_op jit(solution)/shard_map/pallas_call | solution.py:392
  50.6 0.7 %copy.10 = f32[1,3,64,256]{3,2,1,0:T(8,128)} copy(f32[1,3,64,256]{3,2,1,0:T(8,128)S(1)} %get-tuple-element.4) | data formatting | bytes 393216
  51.3 0.7 %copy.11 = f32[3,3,16,256]{3,2,1,0:T(8,128)} copy(f32[3,3,16,256]{3,2,1,0:T(8,128)S(1)} %get-tuple-element.5) | data formatting | bytes 294912
Async XLA Ops:
  0.6 0.7 %copy-start.5 = (f32[256]{0:T(256)S(1)}, f32[256]{0:T(256)}, u32[]{:S(2)}) copy-start(f32[256]{0:T(256)} %param.9) | copy-start | bytes 3076
  1.3 1.1 %copy-start = (f32[3,3,64,256]{3,2,1,0:T(8,128)S(1)}, f32[3,3,64,256]{3,2,1,0:T(8,128)}, u32[]{:S(2)}) copy-start(f32[3,3,64,256]{3,2,1,0:T(8,128)} %coup_in.1) | copy-start | bytes 1769476
  2.4 0.9 %copy-start.1 = (f32[1,3,64,256]{3,2,1,0:T(8,128)S(1)}, f32[1,3,64,256]{3,2,1,0:T(8,128)}, u32[]{:S(2)}) copy-start(f32[1,3,64,256]{3,2,1,0:T(8,128)} %amp_in.1) | copy-start | bytes 589828
  3.3 0.9 %copy-start.2 = (f32[3,64,256]{2,1,0:T(8,128)S(1)}, f32[3,64,256]{2,1,0:T(8,128)}, u32[]{:S(2)}) copy-start(f32[3,64,256]{2,1,0:T(8,128)} %mask_in.1) | copy-start | bytes 589828
  4.2 0.7 %copy-start.3 = (f32[16,256]{1,0:T(8,128)S(1)}, f32[16,256]{1,0:T(8,128)}, u32[]{:S(2)}) copy-start(f32[16,256]{1,0:T(8,128)} %constant.4.clone.table_in) | copy-start | bytes 49156
  4.9 0.7 %copy-start.4 = (f32[16,128]{1,0:T(8,128)S(1)}, f32[16,128]{1,0:T(8,128)}, u32[]{:S(2)}) copy-start(f32[16,128]{1,0:T(8,128)} %constant.5.clone.scaled_in) | copy-start | bytes 24580

commit v3 on v2

--- a/solution.py
+++ b/solution.py
@@ -46,8 +46,8 @@
 def kernel(
     spaces, probes, total_sites,
     amp_in, mask_in, coup_in, target_in, table_in, scaled_in,
-    costate, grad,
-    amp, mask, coup, target, table, scaled,
+    costate_out, grad_out,
+    costate, grad, amp, mask, coup, target, table, scaled,
     v, du, q, g, bond, pair, give, got, mom_a, mom_b, recv, direct,
     load_sem, edge_send, edge_recv, mid_send, mid_recv,
     give_send, give_recv, pass_send, pass_recv,
@@ -275,25 +275,6 @@
     weights, sums = None, None
     for t in range(STEPS - 1):
         low_mid[t].wait_recv()
-        step(t, 1)
-        step(t + 1, first)
-        high_mid[t].wait_recv()
-        step(t, high)
-        step(t + 1, last)
-        if t + 2 < STEPS:
-            step(t + 2, middle)
-        if t + 3 < STEPS - 1:
-            send_middle(t + 3)
-
-        if t < 3:
-            moment(2 * t + 3, t + 1, t + 2)
-            moment(2 * t + 4, t + 2, t + 2)
-        if t == 2:
-            for off in range(1, probes):
-                a_copies.append(send(
-                    mom_a.at[p], mom_a.at[p], ma_send.at[off], ma_recv.at[off],
-                    {"probe": lax.rem(p + off, probes)},
-                ))
         if t == 3:
             for copy in a_copies:
                 copy.wait_recv()
@@ -306,6 +287,27 @@
                     mom_b.at[s], mom_b.at[s], mb_send.at[off], mb_recv.at[off],
                     {"space": lax.rem(s + off, spaces)},
                 ))
+        step(t, 1)
+        step(t + 1, first)
+        high_mid[t].wait_recv()
+        step(t, high)
+        step(t + 1, last)
+        if t == 2:
+            moment(7, 3, 4)
+            moment(8, 4, 4)
+            for off in range(1, probes):
+                a_copies.append(send(
+                    mom_a.at[p], mom_a.at[p], ma_send.at[off], ma_recv.at[off],
+                    {"probe": lax.rem(p + off, probes)},
+                ))
+        if t + 2 < STEPS:
+            step(t + 2, middle)
+        if t + 3 < STEPS - 1:
+            send_middle(t + 3)
+
+        if t < 2:
+            moment(2 * t + 3, t + 1, t + 2)
+            moment(2 * t + 4, t + 2, t + 2)
         if t < STEPS - 2:
             products(t + 1)
         if t == STEPS - 3:
@@ -364,6 +366,8 @@
         ))
     for i in range(planes):
         costate[0, i] = costate[0, i] + 2.0 * weights[STEPS] * v[STEPS, first + i]
+    costate_copy = pltpu.make_async_copy(costate, costate_out, load_sem.at[6])
+    costate_copy.start()
     for level in range(1, levels):
         rs_finish(level)
         if level + 1 < levels:
@@ -375,8 +379,12 @@
         d_copies[off - 1].wait_recv()
         acc = acc + direct[off - 1]
     grad[0, planes - 1] = acc
+    grad_copy = pltpu.make_async_copy(grad, grad_out, load_sem.at[7])
+    grad_copy.start()
     for copy in started:
         copy.wait_send()
+    costate_copy.wait()
+    grad_copy.wait()
 
 
 def on_device(probe_amplitudes, site_mask, couplings, target):
@@ -387,7 +395,6 @@
     levels = probes.bit_length() - 1
     f32 = jnp.float32
     total_sites = float(probes * spaces * planes * rows * lanes)
-    vmem = pl.BlockSpec(memory_space=pltpu.VMEM)
     dma = pltpu.SemaphoreType.DMA
     return pl.pallas_call(
         functools.partial(kernel, spaces, probes, total_sites),
@@ -395,9 +402,11 @@
             jax.ShapeDtypeStruct((1, planes, rows, lanes), f32),
             jax.ShapeDtypeStruct((3, planes, block, lanes), f32),
         ),
-        in_specs=[pl.BlockSpec(memory_space=pl.ANY)] * 6,
-        out_specs=(vmem, vmem),
+        in_specs=[pl.BlockSpec(memory_space=pltpu.HBM)] * 6,
+        out_specs=(pl.BlockSpec(memory_space=pltpu.HBM),) * 2,
         scratch_shapes=[
+            pltpu.VMEM((1, planes, rows, lanes), f32),
+            pltpu.VMEM((3, planes, block, lanes), f32),
             pltpu.VMEM(probe_amplitudes.shape, f32),
             pltpu.VMEM(site_mask.shape, f32),
             pltpu.VMEM(couplings.shape, f32),
@@ -416,14 +425,14 @@
             pltpu.VMEM((spaces, ROWS, LANES), f32),
             pltpu.VMEM((levels, probes // 2, 3 * planes - 1, block, lanes), f32),
             pltpu.VMEM((probes - 1, block, lanes), f32),
-            dma((6,)), dma((2,)), dma((2,)), dma((STEPS, 2)), dma((STEPS, 2)),
+            dma((8,)), dma((2,)), dma((2,)), dma((STEPS, 2)), dma((STEPS, 2)),
             dma((2, 2)), dma((2, 2)), dma((2, 2)), dma((2, 2)),
             dma((probes,)), dma((probes,)), dma((spaces,)), dma((spaces,)),
             dma((levels, probes // 2)), dma((levels, probes // 2)),
             dma((probes,)), dma((probes,)),
         ],
         compiler_params=pltpu.CompilerParams(
-            collective_id=0, has_side_effects=True, vmem_limit_bytes=48 * 1024 * 1024
+            collective_id=0, has_side_effects=True, vmem_limit_bytes=64 * 1024 * 1024
         ),
     )(probe_amplitudes, site_mask, couplings, target[None], table, scaled)
 

time: 52.3 us -> 45.2 us (0.86)
  local copies, waits for them, and re-layouts: 6.34 us -> 2.32 us
  Pallas kernels: 45 us -> 42.1 us
    unnamed x14 -> x4, local copies, waits for them, and re-layouts: 6.34 us -> 2.32 us
    pallas_call x1, Pallas kernels: 45 us -> 42.1 us  [on_device(): pl.pallas_call(functools.partial(kernel, spaces, probes, total_sites), ou...]
where the time goes in v3:
time: 45.2 us; the launch traced here: 45.1 us
  Pallas kernels  42.1 us (93%)
  local copies, waits for them, and re-layouts  2.32 us (5%)
  between operations  0.65 us (1%)
    pallas_call x1, Pallas kernels, on_device(): pl.pallas_call(functools.partial(kernel, spaces, probes, total_sites), ou...  42.1 us
    unnamed x4, local copies, waits for them, and re-layouts  2.32 us

profile of v3, /device:TPU:0, one launch (start us, length us, event | category | flops | bytes accessed | tf_op | source)
XLA Modules:
  0.0 45.1 jit_solution(6008726870903563502)
XLA Ops:
  0.6 42.1 %shard_map.77 = (f32[1,3,64,256]{3,2,1,0:T(8,128)}, f32[3,3,16,256]{3,2,1,0:T(8,128)}) custom-call(f32[1,3,64,256]{3,2,1,0:T(8,128)} %amp_in.1, f32[3,64,256]{2,1,0:T(8,128)} %mask_in.1, f32[3,3,64,256]{3,2,1,0:T(8,128)} %coup_in.1, f32[1,256]{1,0:T(1,128)} %bitcast.1, f32[16,256]{1,0:T(8,128)} %constant.4.clone.table_in, f32[16,128]{1,0:T(8,128)} %constant.5.clone.scaled_in), custom_call_target="tpu_custom_call" | custom-call | tf_op jit(solution)/shard_map/pallas_call | solution.py:399
  42.7 0.0 copy-start
  42.8 1.7 %copy.10 = f32[1,3,64,256]{3,2,1,0:T(8,128)} copy(f32[1,3,64,256]{3,2,1,0:T(8,128)} %get-tuple-element.4) | data formatting | bytes 393216
  44.4 0.0 copy-done
  44.4 0.7 %copy.11 = f32[3,3,16,256]{3,2,1,0:T(8,128)} copy(f32[3,3,16,256]{3,2,1,0:T(8,128)S(1)} %copy-done) | data formatting | bytes 294912
Async XLA Ops:
  42.7 1.7 %copy-start = (f32[3,3,16,256]{3,2,1,0:T(8,128)S(1)}, f32[3,3,16,256]{3,2,1,0:T(8,128)}, u32[]{:S(2)}) copy-start(f32[3,3,16,256]{3,2,1,0:T(8,128)} %get-tuple-element.5) | copy-start | bytes 442372

commit v4 on v3

--- a/solution.py
+++ b/solution.py
@@ -63,13 +63,6 @@
     after, before = lax.rem(s + 1, spaces), lax.rem(s + spaces - 1, spaces)
     twin = flipped(p, 1)
 
-    loads = []
-    for n, (src, dst) in enumerate([
-        (mask_in, mask), (amp_in, amp), (coup_in, coup),
-        (target_in, target), (table_in, table), (scaled_in, scaled),
-    ]):
-        loads.append(pltpu.make_async_copy(src, dst, load_sem.at[n]))
-        loads[-1].start()
     barrier = pltpu.get_barrier_semaphore()
     for off in range(1, spaces):
         pl.semaphore_signal(
@@ -79,6 +72,14 @@
         pl.semaphore_signal(
             barrier, inc=1, device_id={"probe": lax.rem(p + off, probes)}, device_id_type=MESH
         )
+
+    loads = []
+    for n, (src, dst) in enumerate([
+        (mask_in, mask), (amp_in, amp), (coup_in, coup),
+        (target_in, target), (table_in, table), (scaled_in, scaled),
+    ]):
+        loads.append(pltpu.make_async_copy(src, dst, load_sem.at[n]))
+        loads[-1].start()
 
     started = []
 
@@ -218,35 +219,46 @@
         for d, i in every:
             q[n, place(d, i)] = product(n, d, i)
 
+    def gradient_before(d, i, sums):
+        acc = sums[1] * q[0, place(d, i)]
+        for n in range(1, STEPS - 2):
+            acc = acc + sums[n + 1] * q[n, place(d, i)]
+        g[place(d, i)] = acc
+
     def gradient(d, i, sums):
-        acc = sums[STEPS] * product(STEPS - 1, d, i)
-        for n in range(STEPS - 1):
-            acc = acc + sums[n + 1] * q[n, place(d, i)]
+        acc = g[place(d, i)]
+        for n in (STEPS - 2, STEPS - 1):
+            acc = acc + sums[n + 1] * product(n, d, i)
         g[place(d, i)] = pair[d, i] * acc
 
     def rows_of(index):
         return pl.ds(pl.multiple_of(index * block, block), block)
 
     levels = probes.bit_length() - 1
+    parts = ((0, early // 2), (early // 2, early))
     rs_copies = {}
 
-    def rs_start(level):
+    def rs_start(level, part):
         bit = 1 << level
         other = flipped(p, bit)
-        rs_copies[level] = []
+        start, stop = parts[part]
+        rs_copies[level, part] = []
         for j in range(probes // (2 * bit)):
             index = lax.rem(other, 2 * bit) + j * 2 * bit
-            rs_copies[level].append(send(
-                g.at[pl.ds(0, early), rows_of(index)], recv.at[level, j],
-                rs_send.at[level, j], rs_recv.at[level, j], {"probe": other},
+            rs_copies[level, part].append(send(
+                g.at[pl.ds(start, stop - start), rows_of(index)],
+                recv.at[level, j, pl.ds(start, stop - start)],
+                rs_send.at[level, j, part], rs_recv.at[level, j, part], {"probe": other},
             ))
 
-    def rs_finish(level):
+    def rs_finish(level, part):
         bit = 1 << level
-        for j, copy in enumerate(rs_copies[level]):
+        start, stop = parts[part]
+        here = pl.ds(start, stop - start)
+        for j, copy in enumerate(rs_copies[level, part]):
             copy.wait_recv()
             index = lax.rem(p, 2 * bit) + j * 2 * bit
-            g[pl.ds(0, early), rows_of(index)] = g[pl.ds(0, early), rows_of(index)] + recv[level, j]
+            g[here, rows_of(index)] = g[here, rows_of(index)] + recv[level, j, here]
 
     step(0, middle)
     send_middle(1)
@@ -273,7 +285,7 @@
 
     a_copies, b_copies = [], []
     weights, sums = None, None
-    for t in range(STEPS - 1):
+    for t in range(STEPS - 2):
         low_mid[t].wait_recv()
         if t == 3:
             for copy in a_copies:
@@ -300,7 +312,7 @@
                     mom_a.at[p], mom_a.at[p], ma_send.at[off], ma_recv.at[off],
                     {"probe": lax.rem(p + off, probes)},
                 ))
-        if t + 2 < STEPS:
+        if t + 2 < STEPS - 1:
             step(t + 2, middle)
         if t + 3 < STEPS - 1:
             send_middle(t + 3)
@@ -308,9 +320,9 @@
         if t < 2:
             moment(2 * t + 3, t + 1, t + 2)
             moment(2 * t + 4, t + 2, t + 2)
-        if t < STEPS - 2:
+        if t < STEPS - 3:
             products(t + 1)
-        if t == STEPS - 3:
+        if t == STEPS - 4:
             for n in (3, 4, 5):
                 loads[n].wait()
             for copy in b_copies:
@@ -335,6 +347,9 @@
             sums = [None] * (STEPS + 1)
             for n in range(STEPS, 0, -1):
                 sums[n] = weights[n] if n + 2 > STEPS else weights[n] + sums[n + 2]
+            for d, i in every:
+                gradient_before(d, i, sums)
+        if t == STEPS - 3:
             k = STEPS - 1
             for i in range(planes):
                 here = v[k, first + i]
@@ -342,19 +357,24 @@
                 du[2, k, i] = 2.0 * (here - following(here, 1))
                 if i < planes - 1:
                     du[0, k, i] = 2.0 * (here - v[k, first + i + 1])
-            for d, i in every[:-1]:
-                gradient(d, i, sums)
-            rs_start(0)
+            for part, (start, stop) in enumerate(parts):
+                for d, i in every[start:stop]:
+                    gradient(d, i, sums)
+                rs_start(0, part)
+            step(t + 2, middle)
             for i in range(planes):
                 acc = weights[0] * v[0, first + i]
                 for n in range(1, STEPS):
                     acc = acc + weights[n] * v[n, first + i]
-                costate[0, i] = 2.0 * acc
-            rs_finish(0)
-            if levels > 1:
-                rs_start(1)
+                costate[0, i] = acc
+            for part in range(len(parts)):
+                rs_finish(0, part)
+                if levels > 1:
+                    rs_start(1, part)
 
     k = STEPS - 1
+    high_mid[k - 1].wait_recv()
+    step(k - 1, high)
     du[0, k, planes - 1] = 2.0 * (v[k, last] - v[k, high])
     gradient(0, planes - 1, sums)
     d_copies = []
@@ -364,14 +384,19 @@
             g.at[early, rows_of(other)], direct.at[off - 1], d_send.at[off], d_recv.at[off],
             {"probe": other},
         ))
+    step(k, last)
+    low_mid[k - 1].wait_recv()
+    step(k - 1, 1)
+    step(k, first)
     for i in range(planes):
-        costate[0, i] = costate[0, i] + 2.0 * weights[STEPS] * v[STEPS, first + i]
+        costate[0, i] = costate[0, i] + weights[STEPS] * v[STEPS, first + i]
     costate_copy = pltpu.make_async_copy(costate, costate_out, load_sem.at[6])
     costate_copy.start()
     for level in range(1, levels):
-        rs_finish(level)
-        if level + 1 < levels:
-            rs_start(level + 1)
+        for part in range(len(parts)):
+            rs_finish(level, part)
+            if level + 1 < levels:
+                rs_start(level + 1, part)
     for d, i in every[:-1]:
         grad[d, i] = g[place(d, i), rows_of(p)]
     acc = g[early, rows_of(p)]
@@ -396,7 +421,7 @@
     f32 = jnp.float32
     total_sites = float(probes * spaces * planes * rows * lanes)
     dma = pltpu.SemaphoreType.DMA
-    return pl.pallas_call(
+    costate, grad = pl.pallas_call(
         functools.partial(kernel, spaces, probes, total_sites),
         out_shape=(
             jax.ShapeDtypeStruct((1, planes, rows, lanes), f32),
@@ -428,13 +453,14 @@
             dma((8,)), dma((2,)), dma((2,)), dma((STEPS, 2)), dma((STEPS, 2)),
             dma((2, 2)), dma((2, 2)), dma((2, 2)), dma((2, 2)),
             dma((probes,)), dma((probes,)), dma((spaces,)), dma((spaces,)),
-            dma((levels, probes // 2)), dma((levels, probes // 2)),
+            dma((levels, probes // 2, 2)), dma((levels, probes // 2, 2)),
             dma((probes,)), dma((probes,)),
         ],
         compiler_params=pltpu.CompilerParams(
             collective_id=0, has_side_effects=True, vmem_limit_bytes=64 * 1024 * 1024
         ),
     )(probe_amplitudes, site_mask, couplings, target[None], table, scaled)
+    return 2.0 * costate, grad
 
 
 def solution(mesh):

time: 45.2 us -> 45.6 us (level)
  other arithmetic: 0 us -> 1.66 us
  local copies, waits for them, and re-layouts: 2.32 us -> 0.67 us
    mul x0 -> x1, other arithmetic: none -> 1.66 us  [on_device(): return (2.0 * costate, grad)]
    unnamed x4 -> x3, local copies, waits for them, and re-layouts: 2.32 us -> 0.67 us
where the time goes in v4:
time: 45.6 us; the launch traced here: 45.4 us
  Pallas kernels  42.4 us (93%)
  other arithmetic  1.66 us (4%)
  local copies, waits for them, and re-layouts  0.67 us (1%)
  between operations  0.65 us (1%)
    pallas_call x1, Pallas kernels, on_device(): pl.pallas_call(functools.partial(kernel, spaces, probes, total_sites), ou...  42.4 us
    mul x1, other arithmetic, on_device(): return (2.0 * costate, grad)  1.66 us

profile of v4, /device:TPU:0, one launch (start us, length us, event | category | flops | bytes accessed | tf_op | source)
XLA Modules:
  0.0 45.4 jit_solution(10177105980882428995)
XLA Ops:
  0.6 42.4 %shard_map.77 = (f32[1,3,64,256]{3,2,1,0:T(8,128)}, f32[3,3,16,256]{3,2,1,0:T(8,128)}) custom-call(f32[1,3,64,256]{3,2,1,0:T(8,128)} %amp_in.1, f32[3,64,256]{2,1,0:T(8,128)} %mask_in.1, f32[3,3,64,256]{3,2,1,0:T(8,128)} %coup_in.1, f32[1,256]{1,0:T(1,128)} %bitcast.1, f32[16,256]{1,0:T(8,128)} %constant.6.clone.table_in, f32[16,128]{1,0:T(8,128)} %constant.7.clone.scaled_in), custom_call_target="tpu_custom_call" | custom-call | tf_op jit(solution)/shard_map/pallas_call | solution.py:424
  43.1 0.0 copy-start
  43.1 1.7 %broadcast_multiply_fusion = f32[1,3,64,256]{3,2,1,0:T(8,128)} fusion(f32[1,3,64,256]{3,2,1,0:T(8,128)} %get-tuple-element.4), kind=kLoop, calls=%fused_computation | loop fusion | flops 49152 | bytes 393216 | tf_op jit(solution)/shard_map/mul | solution.py:463
  44.8 0.0 copy-done
  44.8 0.7 %copy.9 = f32[3,3,16,256]{3,2,1,0:T(8,128)} copy(f32[3,3,16,256]{3,2,1,0:T(8,128)S(1)} %copy-done) | data formatting | bytes 294912
Async XLA Ops:
  43.1 1.7 %copy-start = (f32[3,3,16,256]{3,2,1,0:T(8,128)S(1)}, f32[3,3,16,256]{3,2,1,0:T(8,128)}, u32[]{:S(2)}) copy-start(f32[3,3,16,256]{3,2,1,0:T(8,128)} %get-tuple-element.9) | copy-start | bytes 442372

commit v5 on v4

--- a/solution.py
+++ b/solution.py
@@ -46,8 +46,8 @@
 def kernel(
     spaces, probes, total_sites,
     amp_in, mask_in, coup_in, target_in, table_in, scaled_in,
-    costate_out, grad_out,
-    costate, grad, amp, mask, coup, target, table, scaled,
+    costate, grad,
+    amp, mask, coup, target, table, scaled,
     v, du, q, g, bond, pair, give, got, mom_a, mom_b, recv, direct,
     load_sem, edge_send, edge_recv, mid_send, mid_recv,
     give_send, give_recv, pass_send, pass_recv,
@@ -104,26 +104,38 @@
 
     own_half = pl.ds(pl.multiple_of(lax.rem(p, 2) * half, half), half)
 
-    def send_bonds(group, start, size):
+    levels = probes.bit_length() - 1
+    turned = sum(lax.rem(lax.div(p, 1 << i), 2) * (1 << (levels - 1 - i)) for i in range(levels))
+
+    def shared_rows(level):
+        size = block << level
+        return pl.ds(pl.multiple_of(lax.div(turned, 1 << level) * size, size), size)
+
+    def send_bonds(group, start, size, rows):
         out = []
         for side, where in ((0, after), (1, before)):
             out.append(send(
-                give.at[side, pl.ds(start, size), own_half],
-                got.at[side, pl.ds(start, size), own_half],
+                give.at[side, pl.ds(start, size), rows],
+                got.at[side, pl.ds(start, size), rows],
                 give_send.at[group, side], give_recv.at[group, side], {"space": where},
             ))
         return out
 
-    def pass_bonds(group, start, size, copies):
+    def pass_bonds(slot, start, size, rows, where, copies):
         out = []
         for side in (0, 1):
             copies[side].wait_recv()
             out.append(send(
-                got.at[side, pl.ds(start, size), own_half],
-                got.at[side, pl.ds(start, size), own_half],
-                pass_send.at[group, side], pass_recv.at[group, side], {"probe": twin},
+                got.at[side, pl.ds(start, size), rows],
+                got.at[side, pl.ds(start, size), rows],
+                pass_send.at[slot, side], pass_recv.at[slot, side], {"probe": where},
             ))
         return out
+
+    def pass_far(level, copies):
+        return pass_bonds(
+            1 + level, 1, 3, shared_rows(level), flipped(p, probes >> (level + 1)), copies
+        )
 
     for n in (0, 1):
         loads[n].wait()
@@ -133,27 +145,29 @@
     edge_low = send(v.at[0, last], v.at[0, 1], edge_send.at[0], edge_recv.at[0], {"space": after})
     edge_high = send(v.at[0, first], v.at[0, high], edge_send.at[1], edge_recv.at[1], {"space": before})
     loads[2].wait()
-    give[0, 0] = (2.0 / SCALE) * (coup[0, planes - 1] * mask[planes - 1])
-    give[1, 0] = mask[0]
-    near = send_bonds(0, 0, 1)
-    send_middle(0)
-
-    for i in range(planes):
-        m = mask[i]
-        tenth = m * (1.0 / SCALE)
-        if i < planes - 1:
-            pair[0, i] = tenth * mask[i + 1]
-            bond[0, first + i] = 2.0 * coup[0, i] * pair[0, i]
-        pair[1, i] = tenth * following(m, 0)
-        pair[2, i] = tenth * following(m, 1)
-        for d in (1, 2):
-            bond[d, first + i] = 2.0 * coup[d, i] * pair[d, i]
+
+    def across(d, i):
+        pair[d, i] = mask[i] * (1.0 / SCALE) * following(mask[i], d - 1)
+        bond[d, first + i] = 2.0 * coup[d, i] * pair[d, i]
+
+    for i in range(planes - 1):
+        pair[0, i] = mask[i] * (1.0 / SCALE) * mask[i + 1]
+        bond[0, first + i] = 2.0 * coup[0, i] * pair[0, i]
     give[0, 1] = bond[0, last - 1]
     give[1, 1] = bond[0, first]
     for d in (1, 2):
+        for i in (0, planes - 1):
+            across(d, i)
         give[0, d + 1] = bond[d, last]
         give[1, d + 1] = bond[d, first]
-    far = send_bonds(1, 1, 3)
+    far = send_bonds(1, 1, 3, shared_rows(0))
+    give[0, 0] = (2.0 / SCALE) * (coup[0, planes - 1] * mask[planes - 1])
+    give[1, 0] = mask[0]
+    near = send_bonds(0, 0, 1, own_half)
+    send_middle(0)
+    for d in (1, 2):
+        for i in range(1, planes - 1):
+            across(d, i)
 
     def strength(d, j):
         if d == 0 and j == 0:
@@ -234,7 +248,6 @@
     def rows_of(index):
         return pl.ds(pl.multiple_of(index * block, block), block)
 
-    levels = probes.bit_length() - 1
     parts = ((0, early // 2), (early // 2, early))
     rs_copies = {}
 
@@ -262,7 +275,8 @@
 
     step(0, middle)
     send_middle(1)
-    near = pass_bonds(0, 0, 1, near)
+    far = pass_far(0, far)
+    near = pass_bonds(0, 0, 1, own_half, twin, near)
     mom_a[p, pl.ds(8, 8), :] = jnp.zeros((8, LANES), jnp.float32)
     moment(0, 0, 0)
     for copy in near:
@@ -276,7 +290,8 @@
     step(0, last)
     step(1, middle)
     send_middle(2)
-    far = pass_bonds(1, 1, 3, far)
+    for level in range(1, levels):
+        far = pass_far(level, far)
     moment(1, 0, 1)
     moment(2, 1, 1)
     products(0)
@@ -366,7 +381,7 @@
                 acc = weights[0] * v[0, first + i]
                 for n in range(1, STEPS):
                     acc = acc + weights[n] * v[n, first + i]
-                costate[0, i] = acc
+                costate[0, i] = 2.0 * acc
             for part in range(len(parts)):
                 rs_finish(0, part)
                 if levels > 1:
@@ -389,9 +404,7 @@
     step(k - 1, 1)
     step(k, first)
     for i in range(planes):
-        costate[0, i] = costate[0, i] + weights[STEPS] * v[STEPS, first + i]
-    costate_copy = pltpu.make_async_copy(costate, costate_out, load_sem.at[6])
-    costate_copy.start()
+        costate[0, i] = costate[0, i] + 2.0 * weights[STEPS] * v[STEPS, first + i]
     for level in range(1, levels):
         for part in range(len(parts)):
             rs_finish(level, part)
@@ -404,12 +417,8 @@
         d_copies[off - 1].wait_recv()
         acc = acc + direct[off - 1]
     grad[0, planes - 1] = acc
-    grad_copy = pltpu.make_async_copy(grad, grad_out, load_sem.at[7])
-    grad_copy.start()
     for copy in started:
         copy.wait_send()
-    costate_copy.wait()
-    grad_copy.wait()
 
 
 def on_device(probe_amplitudes, site_mask, couplings, target):
@@ -424,14 +433,12 @@
     costate, grad = pl.pallas_call(
         functools.partial(kernel, spaces, probes, total_sites),
         out_shape=(
-            jax.ShapeDtypeStruct((1, planes, rows, lanes), f32),
-            jax.ShapeDtypeStruct((3, planes, block, lanes), f32),
+            pltpu.VMEM((1, planes, rows, lanes), f32),
+            pltpu.VMEM((3, planes, block, lanes), f32),
         ),
         in_specs=[pl.BlockSpec(memory_space=pltpu.HBM)] * 6,
-        out_specs=(pl.BlockSpec(memory_space=pltpu.HBM),) * 2,
+        out_specs=(pl.BlockSpec(memory_space=pltpu.VMEM),) * 2,
         scratch_shapes=[
-            pltpu.VMEM((1, planes, rows, lanes), f32),
-            pltpu.VMEM((3, planes, block, lanes), f32),
             pltpu.VMEM(probe_amplitudes.shape, f32),
             pltpu.VMEM(site_mask.shape, f32),
             pltpu.VMEM(couplings.shape, f32),
@@ -450,17 +457,17 @@
             pltpu.VMEM((spaces, ROWS, LANES), f32),
             pltpu.VMEM((levels, probes // 2, 3 * planes - 1, block, lanes), f32),
             pltpu.VMEM((probes - 1, block, lanes), f32),
-            dma((8,)), dma((2,)), dma((2,)), dma((STEPS, 2)), dma((STEPS, 2)),
-            dma((2, 2)), dma((2, 2)), dma((2, 2)), dma((2, 2)),
+            dma((6,)), dma((2,)), dma((2,)), dma((STEPS, 2)), dma((STEPS, 2)),
+            dma((2, 2)), dma((2, 2)), dma((1 + levels, 2)), dma((1 + levels, 2)),
             dma((probes,)), dma((probes,)), dma((spaces,)), dma((spaces,)),
             dma((levels, probes // 2, 2)), dma((levels, probes // 2, 2)),
             dma((probes,)), dma((probes,)),
         ],
         compiler_params=pltpu.CompilerParams(
-            collective_id=0, has_side_effects=True, vmem_limit_bytes=64 * 1024 * 1024
+            collective_id=0, has_side_effects=True, vmem_limit_bytes=63 * 1024 * 1024
         ),
     )(probe_amplitudes, site_mask, couplings, target[None], table, scaled)
-    return 2.0 * costate, grad
+    return costate, grad
 
 
 def solution(mesh):

time: 45.6 us -> 42 us (0.921)
  Pallas kernels: 42.4 us -> 39.9 us
  other arithmetic: 1.66 us -> 0 us
  local copies, waits for them, and re-layouts: 0.67 us -> 1.34 us
    pallas_call x1, Pallas kernels: 42.4 us -> 39.9 us  [on_device(): pl.pallas_call(functools.partial(kernel, spaces, probes, total_sites), ou...]
    mul x1 -> x0, other arithmetic: 1.66 us -> none  [on_device(): return (2.0 * costate, grad)]
    unnamed x3 -> x2, local copies, waits for them, and re-layouts: 0.67 us -> 1.34 us
where the time goes in v5:
time: 42 us; the launch traced here: 41.8 us
  Pallas kernels  39.9 us (95%)
  local copies, waits for them, and re-layouts  1.34 us (3%)
  between operations  0.64 us (2%)
    pallas_call x1, Pallas kernels, on_device(): pl.pallas_call(functools.partial(kernel, spaces, probes, total_sites), ou...  39.9 us
    unnamed x2, local copies, waits for them, and re-layouts  1.34 us

profile of v5, /device:TPU:0, one launch (start us, length us, event | category | flops | bytes accessed | tf_op | source)
XLA Modules:
  0.0 41.8 jit_solution(4445813696342214039)
XLA Ops:
  0.6 39.9 %shard_map.77 = (f32[1,3,64,256]{3,2,1,0:T(8,128)S(1)}, f32[3,3,16,256]{3,2,1,0:T(8,128)S(1)}) custom-call(f32[1,3,64,256]{3,2,1,0:T(8,128)} %amp_in.1, f32[3,64,256]{2,1,0:T(8,128)} %mask_in.1, f32[3,3,64,256]{3,2,1,0:T(8,128)} %coup_in.1, f32[1,256]{1,0:T(1,128)} %bitcast.1, f32[16,256]{1,0:T(8,128)} %constant.4.clone.table_in, ...), custom_call_target="tpu_custom_call" | custom-call | tf_op jit(solution)/shard_map/pallas_call | solution.py:433
  40.5 0.7 %copy.10 = f32[1,3,64,256]{3,2,1,0:T(8,128)} copy(f32[1,3,64,256]{3,2,1,0:T(8,128)S(1)} %get-tuple-element.2) | data formatting | bytes 393216
  41.2 0.7 %copy.11 = f32[3,3,16,256]{3,2,1,0:T(8,128)} copy(f32[3,3,16,256]{3,2,1,0:T(8,128)S(1)} %get-tuple-element.3) | data formatting | bytes 294912

commit v6 on v5

--- a/solution.py
+++ b/solution.py
@@ -64,7 +64,7 @@
     twin = flipped(p, 1)
 
     barrier = pltpu.get_barrier_semaphore()
-    for off in range(1, spaces):
+    for off in [1, spaces - 1, *range(2, spaces - 1)]:
         pl.semaphore_signal(
             barrier, inc=1, device_id={"space": lax.rem(s + off, spaces)}, device_id_type=MESH
         )
@@ -302,18 +302,6 @@
     weights, sums = None, None
     for t in range(STEPS - 2):
         low_mid[t].wait_recv()
-        if t == 3:
-            for copy in a_copies:
-                copy.wait_recv()
-            acc = mom_a[0]
-            for index in range(1, probes):
-                acc = acc + mom_a[index]
-            mom_b[s] = acc
-            for off in range(1, spaces):
-                b_copies.append(send(
-                    mom_b.at[s], mom_b.at[s], mb_send.at[off], mb_recv.at[off],
-                    {"space": lax.rem(s + off, spaces)},
-                ))
         step(t, 1)
         step(t + 1, first)
         high_mid[t].wait_recv()
@@ -337,7 +325,19 @@
             moment(2 * t + 4, t + 2, t + 2)
         if t < STEPS - 3:
             products(t + 1)
-        if t == STEPS - 4:
+        if t == 2:
+            for copy in a_copies:
+                copy.wait_recv()
+            acc = mom_a[0]
+            for index in range(1, probes):
+                acc = acc + mom_a[index]
+            mom_b[s] = acc
+            for off in range(1, spaces):
+                b_copies.append(send(
+                    mom_b.at[s], mom_b.at[s], mb_send.at[off], mb_recv.at[off],
+                    {"space": lax.rem(s + off, spaces)},
+                ))
+        if t == STEPS - 3:
             for n in (3, 4, 5):
                 loads[n].wait()
             for copy in b_copies:
@@ -366,26 +366,23 @@
                 gradient_before(d, i, sums)
         if t == STEPS - 3:
             k = STEPS - 1
-            for i in range(planes):
-                here = v[k, first + i]
-                du[1, k, i] = 2.0 * (here - following(here, 0))
-                du[2, k, i] = 2.0 * (here - following(here, 1))
-                if i < planes - 1:
-                    du[0, k, i] = 2.0 * (here - v[k, first + i + 1])
             for part, (start, stop) in enumerate(parts):
                 for d, i in every[start:stop]:
+                    here = v[k, first + i]
+                    there = v[k, first + i + 1] if d == 0 else following(here, d - 1)
+                    du[d, k, i] = 2.0 * (here - there)
                     gradient(d, i, sums)
                 rs_start(0, part)
             step(t + 2, middle)
+            for part in range(len(parts)):
+                rs_finish(0, part)
+                if levels > 1:
+                    rs_start(1, part)
             for i in range(planes):
                 acc = weights[0] * v[0, first + i]
                 for n in range(1, STEPS):
                     acc = acc + weights[n] * v[n, first + i]
                 costate[0, i] = 2.0 * acc
-            for part in range(len(parts)):
-                rs_finish(0, part)
-                if levels > 1:
-                    rs_start(1, part)
 
     k = STEPS - 1
     high_mid[k - 1].wait_recv()

time: 42 us -> 41.4 us (0.986)
  Pallas kernels: 39.9 us -> 39.2 us
    pallas_call x1, Pallas kernels: 39.9 us -> 39.2 us  [on_device(): pl.pallas_call(functools.partial(kernel, spaces, probes, total_sites), ou...]
where the time goes in v6:
time: 41.4 us; the launch traced here: 41.2 us
  Pallas kernels  39.2 us (95%)
  local copies, waits for them, and re-layouts  1.34 us (3%)
  between operations  0.64 us (2%)
    pallas_call x1, Pallas kernels, on_device(): pl.pallas_call(functools.partial(kernel, spaces, probes, total_sites), ou...  39.2 us
    unnamed x2, local copies, waits for them, and re-layouts  1.34 us

profile of v6, /device:TPU:0, one launch (start us, length us, event | category | flops | bytes accessed | tf_op | source)
XLA Modules:
  0.0 41.2 jit_solution(9294377420643446936)
XLA Ops:
  0.6 39.2 %shard_map.77 = (f32[1,3,64,256]{3,2,1,0:T(8,128)S(1)}, f32[3,3,16,256]{3,2,1,0:T(8,128)S(1)}) custom-call(f32[1,3,64,256]{3,2,1,0:T(8,128)} %amp_in.1, f32[3,64,256]{2,1,0:T(8,128)} %mask_in.1, f32[3,3,64,256]{3,2,1,0:T(8,128)} %coup_in.1, f32[1,256]{1,0:T(1,128)} %bitcast.1, f32[16,256]{1,0:T(8,128)} %constant.4.clone.table_in, ...), custom_call_target="tpu_custom_call" | custom-call | tf_op jit(solution)/shard_map/pallas_call | solution.py:430
  39.9 0.7 %copy.10 = f32[1,3,64,256]{3,2,1,0:T(8,128)} copy(f32[1,3,64,256]{3,2,1,0:T(8,128)S(1)} %get-tuple-element.2) | data formatting | bytes 393216
  40.5 0.7 %copy.11 = f32[3,3,16,256]{3,2,1,0:T(8,128)} copy(f32[3,3,16,256]{3,2,1,0:T(8,128)S(1)} %get-tuple-element.3) | data formatting | bytes 294912
